TPU v7x, 32 devices: a whole 2x2x4 slice. The times are simulated.
32 devices in a mesh: pool: 8 (over z, y), head: 4 (over x, core).
Axes of the slice: x: 2, y: 2, z: 4, core: 2. Of those that a mesh axis runs over, the one named last changes fastest.
Arguments:
- queries: bfloat16 [8, 2048, 8, 128], P('pool', None, 'head'), may hold values from -64 to 64
- new_pairs: bfloat16 [8, 2, 2048, 128], P('pool'), may hold values from -8 to 8
- kv_pool: bfloat16 [1024, 2, 64, 128], P('pool'), may hold values from -6 to 6
- page_owner: int32 [8, 64], P('pool'), may hold values from 0 to 7, as said below
- page_slot: int32 [8, 64], P('pool'), may hold values from 0 to 127, as said below
- prefix_len: int32 [8], P('pool'), may hold values from 2049 to 4096
- fresh_owner: int32 [8, 32], P('pool'), may hold values from 0 to 7, as said below
- fresh_slot: int32 [8, 32], P('pool'), may hold values from 0 to 31, as said below
Outputs:
- attended: bfloat16 [8, 2048, 8, 128], P('pool', None, 'head')
- stored: bfloat16 [256, 2, 64, 128], P('pool')
Inputs may be any that keep to these rules, and one draw needn't show every extreme that they name: `page_owner`: for every request no owner holds more than 16 of the first ceil(prefix_len / 64) pages, and one owner, the same for all requests, holds exactly 16 of them for every request. `page_slot`: each (owner, slot) pair is named by at most one entry over all requests and all 64 entries. `fresh_owner`: for every request no owner receives more than 4 of its new pages, and one owner, the same for all requests, receives exactly 4 from every request. `fresh_slot`: each (owner, slot) pair is named by at most one new page over all requests.
All inputs are finite; a program needn't handle non-finite values.
Results may differ from a plain program's by a relative error of at most 0.0065.
Values may be sent and summed in bfloat16 or wider, within the bound.
A program may use at most 64 MiB of HBM per device.

v0:
```python
import math

import jax
import jax.numpy as jnp
from jax import lax
from jax.sharding import PartitionSpec as P

masked_score = -1e30


def place_cells(owners, slot_ids, is_live, per_owner, pool_count):
    how_many = owners.shape[0]
    indices = jnp.arange(how_many, dtype=jnp.int32)
    earlier = indices[:, None] > indices[None, :]
    same_owner = owners[:, None] == owners[None, :]
    position = jnp.sum(jnp.where(earlier & same_owner & is_live[None, :], 1, 0), axis=1).astype(
        jnp.int32
    )
    cell_ids = jnp.where(is_live, owners * per_owner + position, -1)
    matches = cell_ids[:, None] == jnp.arange(pool_count * per_owner, dtype=jnp.int32)[None, :]
    slot_table = jnp.sum(jnp.where(matches, slot_ids[:, None], 0), axis=0)
    return (cell_ids, matches, slot_table.reshape(pool_count, per_owner))


def prefix_request(owners, slot_ids, length, page_len, per_owner, pool_count):
    live_pages = (length + page_len - 1) // page_len
    is_live = jnp.arange(owners.shape[0], dtype=jnp.int32) < live_pages
    return place_cells(owners, slot_ids, is_live, per_owner, pool_count)


def absorb(state_in, query_rows, key_rows, value_rows, allowed, scaling):
    running_max, running_sum, weighted = state_in
    scores = (
        jnp.einsum("chd,kd->hck", query_rows, key_rows, preferred_element_type=jnp.float32)
        * scaling
    )
    scores = jnp.where(allowed[None, :, :], scores, masked_score)
    new_max = jnp.maximum(running_max, jnp.max(scores, axis=2))
    correction = jnp.exp(running_max - new_max)
    weights = jnp.exp(scores - new_max[:, :, None])
    running_sum = running_sum * correction + jnp.sum(weights, axis=2)
    weighted = weighted * correction[:, :, None] + jnp.einsum(
        "hck,kd->hcd", weights.astype(jnp.bfloat16), value_rows, preferred_element_type=jnp.float32
    )
    return (new_max, running_sum, weighted)


def shards(queries, new_pairs, kv_pool, page_owner, page_slot, prefix_len, fresh_owner, fresh_slot):
    pool_count = lax.axis_size("pool")
    page_len = kv_pool.shape[2]
    head_dim = kv_pool.shape[3]
    max_pages = page_owner.shape[1]
    bucket = 2 * ((max_pages + pool_count - 1) // pool_count)
    new_len = new_pairs.shape[2]
    new_count = new_len // page_len
    write_bound = (new_count + pool_count - 1) // pool_count
    fresh_total = pool_count * write_bound
    length = prefix_len[0]
    pair_rows = new_pairs[0]
    new_pages = pair_rows.reshape(2, new_count, page_len, head_dim).transpose(1, 0, 2, 3)
    every_page = jnp.ones((new_count,), dtype=bool)
    fresh_cells, fresh_matches, dest_table = place_cells(
        fresh_owner[0], fresh_slot[0], every_page, write_bound, pool_count
    )
    source = jnp.sum(
        jnp.where(fresh_matches, jnp.arange(new_count, dtype=jnp.int32)[:, None], 0), axis=0
    )
    filled = jnp.any(fresh_matches, axis=0).reshape(pool_count, write_bound)
    dest_slots = jnp.where(filled, dest_table, fresh_total)
    outgoing = jnp.take(new_pages, source, axis=0).reshape(
        pool_count, write_bound, 2, page_len, head_dim
    )
    arrived, arrived_slots = (
        lax.all_to_all(outgoing, "pool", split_axis=0, concat_axis=0, tiled=True),
        lax.all_to_all(dest_slots, "pool", split_axis=0, concat_axis=0, tiled=True),
    )
    stored = jnp.zeros((fresh_total, 2, outgoing.shape[3], head_dim), jnp.bfloat16)
    stored = stored.at[arrived_slots.reshape(-1)].set(
        arrived.reshape(-1, 2, outgoing.shape[3], head_dim), mode="drop"
    )
    prefix_cells, prefix_matches, request_table = prefix_request(
        page_owner[0], page_slot[0], length, page_len, bucket, pool_count
    )
    fetched = lax.all_to_all(
        kv_pool[lax.all_to_all(request_table, "pool", split_axis=0, concat_axis=0, tiled=True)],
        "pool",
        split_axis=0,
        concat_axis=0,
        tiled=True,
    )
    flattened = fetched.reshape(pool_count * bucket, 2, page_len, head_dim)
    prefix_pages = jnp.take(flattened, jnp.maximum(prefix_cells, 0), axis=0)
    prefix_keys = prefix_pages[:, 0].reshape(-1, head_dim)
    prefix_values = prefix_pages[:, 1].reshape(-1, head_dim)
    query_rows = queries[0]
    scaling = 1.0 / math.sqrt(head_dim)
    head_local = query_rows.shape[1]
    key_total = prefix_keys.shape[0]
    block_len = math.gcd(key_total, 1024)
    initial = (
        jnp.full((head_local, new_len), masked_score, jnp.float32),
        jnp.zeros((head_local, new_len), jnp.float32),
        jnp.zeros((head_local, new_len, head_dim), jnp.float32),
    )

    def advance(block_index, state_in):
        offset = block_index * block_len
        key_rows = lax.dynamic_slice_in_dim(prefix_keys, offset, block_len, 0)
        value_rows = lax.dynamic_slice_in_dim(prefix_values, offset, block_len, 0)
        allowed = (offset + jnp.arange(block_len, dtype=jnp.int32))[None, :] < length
        return absorb(state_in, query_rows, key_rows, value_rows, allowed, scaling)

    block_count = (length + block_len - 1) // block_len
    state = lax.fori_loop(0, block_count, advance, initial)
    positions = jnp.arange(new_len, dtype=jnp.int32)
    new_block = math.gcd(new_len, 1024)

    def advance_new(block_index, state_in):
        offset = block_index * new_block
        key_rows = lax.dynamic_slice_in_dim(pair_rows[0], offset, new_block, 0)
        value_rows = lax.dynamic_slice_in_dim(pair_rows[1], offset, new_block, 0)
        allowed = (offset + jnp.arange(new_block, dtype=jnp.int32))[None, :] <= positions[:, None]
        return absorb(state_in, query_rows, key_rows, value_rows, allowed, scaling)

    running_max, running_sum, weighted = lax.fori_loop(0, new_len // new_block, advance_new, state)
    attended = (weighted / running_sum[:, :, None]).astype(jnp.bfloat16).transpose(1, 0, 2)[None]
    return (attended, stored)


def solution(mesh):
    in_specs = (
        P("pool", None, "head", None),
        P("pool", None, None, None),
        P("pool", None, None, None),
        P("pool", None),
        P("pool", None),
        P("pool"),
        P("pool", None),
        P("pool", None),
    )
    out_specs = (P("pool", None, "head", None), P("pool", None, None, None))
    return jax.shard_map(shards, mesh=mesh, in_specs=in_specs, out_specs=out_specs, check_vma=False)
```

profile of v0, /device:TPU:0, one launch (start us, length us, event | category | flops | bytes accessed | tf_op | source)
XLA Modules:
  0.0 268.0 jit_solution(4729151957486563358)
XLA Ops:
  3.7 7.3 %all-to-all-start.2 = ((s32[8,1,4]{2,1,0:T(1,128)}), s32[8,1,4]{2,1,0:T(1,128)S(1)}, u32[]{:S(2)}, u32[]{:S(2)}) async-start(s32[8,1,4]{2,1,0:T(1,128)} %bitcast.21), calls=%async_computation.2 | async-start | bytes 8192 | tf_op jit(solution)/shard_map/all_to_all | solution.py:75
  14.8 2.0 gather_fusion.2
  17.4 5.4 %all-to-all-start = ((s32[8,1,16]{2,1,0:T(1,128)}), s32[8,1,16]{2,1,0:T(1,128)S(1)}, u32[]{:S(2)}, u32[]{:S(2)}) async-start(s32[8,1,16]{2,1,0:T(1,128)} %bitcast.6), calls=%async_computation | async-start | bytes 8192 | tf_op jit(solution)/shard_map/all_to_all | solution.py:85
  23.9 5.3 %all-to-all-done = s32[8,1,16]{2,1,0:T(1,128)S(1)} async-done(((s32[8,1,16]{2,1,0:T(1,128)}), s32[8,1,16]{2,1,0:T(1,128)S(1)}, u32[]{:S(2)}, u32[]{:S(2)}) %all-to-all-start) | async-done | bytes 544 | tf_op jit(solution)/shard_map/all_to_all | solution.py:85
  29.2 3.6 %all-to-all-start.3 = ((bf16[8,4,2,64,128]{4,3,2,1,0:T(8,128)(2,1)}), bf16[8,4,2,64,128]{4,3,2,1,0:T(8,128)(2,1)S(1)}, u32[]{:S(2)}, u32[]{:S(2)}) async-start(bf16[8,4,2,64,128]{4,3,2,1,0:T(8,128)(2,1)} %broadcast_select_fusion.1), calls=%async_computation.3 | async-start | bytes 2097152 | tf_op jit(solution)/shard_map/all_to_all | solution.py:74
  32.9 5.3 %gather_fusion = bf16[128,2,64,128]{3,2,1,0:T(8,128)(2,1)} fusion(bf16[128,2,64,128]{3,2,1,0:T(8,128)(2,1)} %param.14, s32[1024]{0:T(1024)S(1)} %pad_clamp_fusion.2), kind=kCustom, calls=%fused_computation | custom fusion | bytes 8389120 | tf_op jit(solution)/shard_map/gather | solution.py:85
  38.2 18.7 %all-to-all-done.3 = bf16[8,4,2,64,128]{4,3,2,1,0:T(8,128)(2,1)S(1)} async-done(((bf16[8,4,2,64,128]{4,3,2,1,0:T(8,128)(2,1)}), bf16[8,4,2,64,128]{4,3,2,1,0:T(8,128)(2,1)S(1)}, u32[]{:S(2)}, u32[]{:S(2)}) %all-to-all-start.3) | async-done | bytes 1048608 | tf_op jit(solution)/shard_map/all_to_all | solution.py:74
  56.9 4.5 %all-to-all-start.1 = ((bf16[8,16,2,64,128]{4,3,2,1,0:T(8,128)(2,1)}), bf16[8,16,2,64,128]{4,3,2,1,0:T(8,128)(2,1)}, u32[]{:S(2)}, u32[]{:S(2)}) async-start(bf16[8,16,2,64,128]{4,3,2,1,0:T(8,128)(2,1)} %bitcast.120), calls=%async_computation.1 | async-start | bytes 8388608 | tf_op jit(solution)/shard_map/all_to_all | solution.py:84
  65.0 88.6 %all-to-all-done.1 = bf16[8,16,2,64,128]{4,3,2,1,0:T(8,128)(2,1)} async-done(((bf16[8,16,2,64,128]{4,3,2,1,0:T(8,128)(2,1)}), bf16[8,16,2,64,128]{4,3,2,1,0:T(8,128)(2,1)}, u32[]{:S(2)}, u32[]{:S(2)}) %all-to-all-start.1) | async-done | bytes 4194336 | tf_op jit(solution)/shard_map/all_to_all | solution.py:84
  153.6 3.1 %gather_fusion.1 = bf16[64,2,64,128]{3,2,1,0:T(8,128)(2,1)S(1)} fusion(bf16[128,2,64,128]{3,2,1,0:T(8,128)(2,1)} %bitcast.9, s32[1024]{0:T(1024)S(1)} %pad_clamp_fusion.1), kind=kCustom, calls=%fused_computation.1 | custom fusion | bytes 4194560 | tf_op jit(solution)/shard_map/jit(_take)/gather | solution.py:92
  159.7 61.8 %while.32 = (s32[]{:T(128)}, f32[2,2048]{1,0:T(2,128)S(1)}, f32[2,2048]{1,0:T(2,128)S(1)}, f32[2,2048,128]{2,1,0:T(8,128)}, s32[]{:T(128)}, /*index=5*/s32[]{:T(...) while((s32[]{:T(128)}, f32[2,2048]{1,0:T(2,128)S(1)}, ...), condition=%wide.region_5.6_spmd, body=%wide.region_2.5_spmd.sunk | while | flops 2194679808 | bytes 73142520 | solution.py:114
  160.5 3.1 %bitcast_reduce_fusion.2 = (f32[2,2048]{1,0:T(2,128)S(1)}, f32[1024,2048,2]{1,0,2:T(8,128)S(1)}) fusion(pred[1024]{0:T(1024)(128)(4,1)S(1)} %add_compare_fusion.2, bf16[2048,2,128]{2,0,1:T(8,128)(2,1)S(1)} %get-tuple-element.390, bf16[4096,128]{1,0:T(8,128)(2,1)S(1)} %get-tuple-element.389, s32[]{:T(128)S(6)} %select_n.214), kind=kOutput, calls=%fused_computation.6.clone.1 | convolution fusion | flops 1086320640 | bytes 18105348 | tf_op jit(solution)/shard_map/while/body/chd,kd->hck/dot_general | solution.py:34
  163.6 4.2 %fusion.66 = f32[2,2048]{1,0:T(2,128)S(1)} fusion(f32[1024,2048,2]{1,0,2:T(8,128)S(1)} %get-tuple-element.342, f32[2,2048]{1,0:T(2,128)S(1)} %max.42, pred[1024]{0:T(1024)(128)(4,1)S(1)} %add_compare_fusion.2), kind=kLoop, calls=%fused_computation.10.clone.1 | loop fusion | flops 16773120 | bytes 16811008 | tf_op jit(solution)/shard_map/while/body/reduce_sum | solution.py:41
  167.8 6.1 %fusion.67 = f32[2,2048,128]{2,1,0:T(8,128)S(1)} fusion(f32[1024,2048,2]{1,0,2:T(8,128)S(1)} %get-tuple-element.342, f32[2,2048]{1,0:T(2,128)S(1)} %max.42, pred[1024]{0:T(1024)(128)(4,1)S(1)} %add_compare_fusion.2, f32[2,2048,128]{2,1,0:T(8,128)S(1)} %copy-done.1, f32[2,2048]{1,0:T(2,128)S(1)} %get-tuple-element.344, ...), kind=kOutput, calls=%fused_computation.13.clone.1 | convolution fusion | flops 1091567616 | bytes 21267460 | tf_op jit(solution)/shard_map/while/body/hck,kd->hcd/dot_general | solution.py:42
  175.9 3.1 %bitcast_reduce_fusion.2 = (f32[2,2048]{1,0:T(2,128)S(1)}, f32[1024,2048,2]{1,0,2:T(8,128)S(1)}) fusion(pred[1024]{0:T(1024)(128)(4,1)S(1)} %add_compare_fusion.2, bf16[2048,2,128]{2,0,1:T(8,128)(2,1)S(1)} %get-tuple-element.390, bf16[4096,128]{1,0:T(8,128)(2,1)S(1)} %get-tuple-element.389, s32[]{:T(128)S(6)} %select_n.214), kind=kOutput, calls=%fused_computation.6.clone.1 | convolution fusion | flops 1086320640 | bytes 18105348 | tf_op jit(solution)/shard_map/while/body/chd,kd->hck/dot_general | solution.py:34
  179.1 4.2 %fusion.66 = f32[2,2048]{1,0:T(2,128)S(1)} fusion(f32[1024,2048,2]{1,0,2:T(8,128)S(1)} %get-tuple-element.342, f32[2,2048]{1,0:T(2,128)S(1)} %max.42, pred[1024]{0:T(1024)(128)(4,1)S(1)} %add_compare_fusion.2), kind=kLoop, calls=%fused_computation.10.clone.1 | loop fusion | flops 16773120 | bytes 16811008 | tf_op jit(solution)/shard_map/while/body/reduce_sum | solution.py:41
  183.3 6.1 %fusion.67 = f32[2,2048,128]{2,1,0:T(8,128)S(1)} fusion(f32[1024,2048,2]{1,0,2:T(8,128)S(1)} %get-tuple-element.342, f32[2,2048]{1,0:T(2,128)S(1)} %max.42, pred[1024]{0:T(1024)(128)(4,1)S(1)} %add_compare_fusion.2, f32[2,2048,128]{2,1,0:T(8,128)S(1)} %copy-done.1, f32[2,2048]{1,0:T(2,128)S(1)} %get-tuple-element.344, ...), kind=kOutput, calls=%fused_computation.13.clone.1 | convolution fusion | flops 1091567616 | bytes 21267460 | tf_op jit(solution)/shard_map/while/body/hck,kd->hcd/dot_general | solution.py:42
  191.3 3.1 %bitcast_reduce_fusion.2 = (f32[2,2048]{1,0:T(2,128)S(1)}, f32[1024,2048,2]{1,0,2:T(8,128)S(1)}) fusion(pred[1024]{0:T(1024)(128)(4,1)S(1)} %add_compare_fusion.2, bf16[2048,2,128]{2,0,1:T(8,128)(2,1)S(1)} %get-tuple-element.390, bf16[4096,128]{1,0:T(8,128)(2,1)S(1)} %get-tuple-element.389, s32[]{:T(128)S(6)} %select_n.214), kind=kOutput, calls=%fused_computation.6.clone.1 | convolution fusion | flops 1086320640 | bytes 18105348 | tf_op jit(solution)/shard_map/while/body/chd,kd->hck/dot_general | solution.py:34
  194.5 4.2 %fusion.66 = f32[2,2048]{1,0:T(2,128)S(1)} fusion(f32[1024,2048,2]{1,0,2:T(8,128)S(1)} %get-tuple-element.342, f32[2,2048]{1,0:T(2,128)S(1)} %max.42, pred[1024]{0:T(1024)(128)(4,1)S(1)} %add_compare_fusion.2), kind=kLoop, calls=%fused_computation.10.clone.1 | loop fusion | flops 16773120 | bytes 16811008 | tf_op jit(solution)/shard_map/while/body/reduce_sum | solution.py:41
  198.7 6.1 %fusion.67 = f32[2,2048,128]{2,1,0:T(8,128)S(1)} fusion(f32[1024,2048,2]{1,0,2:T(8,128)S(1)} %get-tuple-element.342, f32[2,2048]{1,0:T(2,128)S(1)} %max.42, pred[1024]{0:T(1024)(128)(4,1)S(1)} %add_compare_fusion.2, f32[2,2048,128]{2,1,0:T(8,128)S(1)} %copy-done.1, f32[2,2048]{1,0:T(2,128)S(1)} %get-tuple-element.344, ...), kind=kOutput, calls=%fused_computation.13.clone.1 | convolution fusion | flops 1091567616 | bytes 21267460 | tf_op jit(solution)/shard_map/while/body/hck,kd->hcd/dot_general | solution.py:42
  206.8 3.1 %bitcast_reduce_fusion.2 = (f32[2,2048]{1,0:T(2,128)S(1)}, f32[1024,2048,2]{1,0,2:T(8,128)S(1)}) fusion(pred[1024]{0:T(1024)(128)(4,1)S(1)} %add_compare_fusion.2, bf16[2048,2,128]{2,0,1:T(8,128)(2,1)S(1)} %get-tuple-element.390, bf16[4096,128]{1,0:T(8,128)(2,1)S(1)} %get-tuple-element.389, s32[]{:T(128)S(6)} %select_n.214), kind=kOutput, calls=%fused_computation.6.clone.1 | convolution fusion | flops 1086320640 | bytes 18105348 | tf_op jit(solution)/shard_map/while/body/chd,kd->hck/dot_general | solution.py:34
  209.9 4.2 %fusion.66 = f32[2,2048]{1,0:T(2,128)S(1)} fusion(f32[1024,2048,2]{1,0,2:T(8,128)S(1)} %get-tuple-element.342, f32[2,2048]{1,0:T(2,128)S(1)} %max.42, pred[1024]{0:T(1024)(128)(4,1)S(1)} %add_compare_fusion.2), kind=kLoop, calls=%fused_computation.10.clone.1 | loop fusion | flops 16773120 | bytes 16811008 | tf_op jit(solution)/shard_map/while/body/reduce_sum | solution.py:41
  214.1 6.1 %fusion.67 = f32[2,2048,128]{2,1,0:T(8,128)S(1)} fusion(f32[1024,2048,2]{1,0,2:T(8,128)S(1)} %get-tuple-element.342, f32[2,2048]{1,0:T(2,128)S(1)} %max.42, pred[1024]{0:T(1024)(128)(4,1)S(1)} %add_compare_fusion.2, f32[2,2048,128]{2,1,0:T(8,128)S(1)} %copy-done.1, f32[2,2048]{1,0:T(2,128)S(1)} %get-tuple-element.344, ...), kind=kOutput, calls=%fused_computation.13.clone.1 | convolution fusion | flops 1091567616 | bytes 21267460 | tf_op jit(solution)/shard_map/while/body/hck,kd->hcd/dot_general | solution.py:42
  221.5 35.0 %while.33 = (s32[]{:T(128)}, f32[2,2048]{1,0:T(2,128)S(1)}, f32[2,2048]{1,0:T(2,128)S(1)}, f32[2,2048,128]{2,1,0:T(8,128)}, bf16[2,2048,128]{2,1,0:T(8,128)(2,1)...) while((s32[]{:T(128)}, f32[2,2048]{1,0:T(2,128)S(1)}, ...), condition=%wide.region_9.10_spmd.clone, body=%wide.region_6.9_spmd.clone.sunk | while | flops 2196775936 | bytes 66855068 | solution.py:125
  223.3 4.2 %fusion.72 = (f32[2,2048]{1,0:T(2,128)S(1)}, f32[1024,2048,2]{1,0,2:T(8,128)S(1)}) fusion(pred[2048,1024]{0,1:T(8,128)(4,1)S(1)} %iota_compare_fusion.7, bf16[2048,2,128]{2,0,1:T(8,128)(2,1)S(1)} %get-tuple-element.421, bf16[1,2048,128]{2,1,0:T(8,128)(2,1)S(1)} %get-tuple-element.351, s32[]{:T(128)S(6)} %select_n.218), kind=kOutput, calls=%fused_computation.30.clone.1 | convolution fusion | flops 1086320640 | bytes 20201476 | tf_op jit(solution)/shard_map/while/body/eval_jaxpr/chd,kd->hck/dot_general | solution.py:34
  227.6 4.0 %fusion.73 = f32[2,2048]{1,0:T(2,128)S(1)} fusion(f32[1024,2048,2]{1,0,2:T(8,128)S(1)} %get-tuple-element.353, f32[2,2048]{1,0:T(2,128)S(1)} %max.43, pred[2048,1024]{0,1:T(8,128)(4,1)S(1)} %iota_compare_fusion.7), kind=kLoop, calls=%fused_computation.29.clone.1 | loop fusion | flops 16773120 | bytes 18907136 | tf_op jit(solution)/shard_map/while/body/eval_jaxpr/reduce_sum | solution.py:41
  231.7 7.4 %fusion.74 = f32[2,2048,128]{2,1,0:T(8,128)} fusion(f32[1024,2048,2]{1,0,2:T(8,128)S(1)} %get-tuple-element.353, f32[2,2048]{1,0:T(2,128)S(1)} %max.43, pred[2048,1024]{0,1:T(8,128)(4,1)S(1)} %iota_compare_fusion.7, f32[2,2048,128]{2,1,0:T(8,128)} %get-tuple-element.409, f32[2,2048]{1,0:T(2,128)S(1)} %get-tuple-element.355, ...), kind=kOutput, calls=%fused_computation.34.clone.1 | convolution fusion | flops 1091567616 | bytes 23363588 | tf_op jit(solution)/shard_map/while/body/eval_jaxpr/hck,kd->hcd/dot_general | solution.py:42
  240.8 4.2 %fusion.72 = (f32[2,2048]{1,0:T(2,128)S(1)}, f32[1024,2048,2]{1,0,2:T(8,128)S(1)}) fusion(pred[2048,1024]{0,1:T(8,128)(4,1)S(1)} %iota_compare_fusion.7, bf16[2048,2,128]{2,0,1:T(8,128)(2,1)S(1)} %get-tuple-element.421, bf16[1,2048,128]{2,1,0:T(8,128)(2,1)S(1)} %get-tuple-element.351, s32[]{:T(128)S(6)} %select_n.218), kind=kOutput, calls=%fused_computation.30.clone.1 | convolution fusion | flops 1086320640 | bytes 20201476 | tf_op jit(solution)/shard_map/while/body/eval_jaxpr/chd,kd->hck/dot_general | solution.py:34
  245.1 4.0 %fusion.73 = f32[2,2048]{1,0:T(2,128)S(1)} fusion(f32[1024,2048,2]{1,0,2:T(8,128)S(1)} %get-tuple-element.353, f32[2,2048]{1,0:T(2,128)S(1)} %max.43, pred[2048,1024]{0,1:T(8,128)(4,1)S(1)} %iota_compare_fusion.7), kind=kLoop, calls=%fused_computation.29.clone.1 | loop fusion | flops 16773120 | bytes 18907136 | tf_op jit(solution)/shard_map/while/body/eval_jaxpr/reduce_sum | solution.py:41
  249.1 7.4 %fusion.74 = f32[2,2048,128]{2,1,0:T(8,128)} fusion(f32[1024,2048,2]{1,0,2:T(8,128)S(1)} %get-tuple-element.353, f32[2,2048]{1,0:T(2,128)S(1)} %max.43, pred[2048,1024]{0,1:T(8,128)(4,1)S(1)} %iota_compare_fusion.7, f32[2,2048,128]{2,1,0:T(8,128)} %get-tuple-element.409, f32[2,2048]{1,0:T(2,128)S(1)} %get-tuple-element.355, ...), kind=kOutput, calls=%fused_computation.34.clone.1 | convolution fusion | flops 1091567616 | bytes 23363588 | tf_op jit(solution)/shard_map/while/body/eval_jaxpr/hck,kd->hcd/dot_general | solution.py:42
  256.5 2.0 fusion.38
  258.5 9.5 %copy.39 = bf16[1,2048,2,128]{3,2,1,0:T(2,128)(2,1)} copy(bf16[1,2048,2,128]{3,1,2,0:T(8,128)(2,1)S(1)} %fusion.38) | data formatting | bytes 2097152
  (86 shorter events, 26.3 us)
Async XLA Ops:
  3.7 13.7 %all-to-all-start.2 = ((s32[8,1,4]{2,1,0:T(1,128)}), s32[8,1,4]{2,1,0:T(1,128)S(1)}, u32[]{:S(2)}, u32[]{:S(2)}) async-start(s32[8,1,4]{2,1,0:T(1,128)} %bitcast.21), calls=%async_computation.2 | async-start | bytes 8192 | tf_op jit(solution)/shard_map/all_to_all | solution.py:75
  17.4 11.8 %all-to-all-start = ((s32[8,1,16]{2,1,0:T(1,128)}), s32[8,1,16]{2,1,0:T(1,128)S(1)}, u32[]{:S(2)}, u32[]{:S(2)}) async-start(s32[8,1,16]{2,1,0:T(1,128)} %bitcast.6), calls=%async_computation | async-start | bytes 8192 | tf_op jit(solution)/shard_map/all_to_all | solution.py:85
  29.2 27.7 %all-to-all-start.3 = ((bf16[8,4,2,64,128]{4,3,2,1,0:T(8,128)(2,1)}), bf16[8,4,2,64,128]{4,3,2,1,0:T(8,128)(2,1)S(1)}, u32[]{:S(2)}, u32[]{:S(2)}) async-start(bf16[8,4,2,64,128]{4,3,2,1,0:T(8,128)(2,1)} %broadcast_select_fusion.1), calls=%async_computation.3 | async-start | bytes 2097152 | tf_op jit(solution)/shard_map/all_to_all | solution.py:74
  32.9 28.6 %copy-start.4 = (bf16[1,2048,2,128]{3,2,1,0:T(2,128)(2,1)S(1)}, bf16[1,2048,2,128]{3,2,1,0:T(2,128)(2,1)}, u32[]{:S(2)}) copy-start(bf16[1,2048,2,128]{3,2,1,0:T(2,128)(2,1)} %param.12) | copy-start | bytes 3145732
  32.9 28.8 %copy-start.5 = (s32[1,64]{1,0:T(1,128)S(1)}, s32[1,64]{1,0:T(1,128)}, u32[]{:S(2)}) copy-start(s32[1,64]{1,0:T(1,128)} %param.15) | copy-start | bytes 772
  56.9 96.7 %all-to-all-start.1 = ((bf16[8,16,2,64,128]{4,3,2,1,0:T(8,128)(2,1)}), bf16[8,16,2,64,128]{4,3,2,1,0:T(8,128)(2,1)}, u32[]{:S(2)}, u32[]{:S(2)}) async-start(bf16[8,16,2,64,128]{4,3,2,1,0:T(8,128)(2,1)} %bitcast.120), calls=%async_computation.1 | async-start | bytes 8388608 | tf_op jit(solution)/shard_map/all_to_all | solution.py:84
  65.0 88.7 %copy-start.3 = (bf16[32,2,64,128]{3,2,1,0:T(8,128)(2,1)}, bf16[32,2,64,128]{3,2,1,0:T(8,128)(2,1)S(1)}, u32[]{:S(2)}) copy-start(bf16[32,2,64,128]{3,2,1,0:T(8,128)(2,1)S(1)} %scatter_fusion) | copy-start | bytes 3145732
  159.7 61.8 %copy-start = (bf16[1,2,2048,128]{3,2,1,0:T(8,128)(2,1)S(1)}, bf16[1,2,2048,128]{3,2,1,0:T(8,128)(2,1)}, u32[]{:S(2)}) copy-start(bf16[1,2,2048,128]{3,2,1,0:T(8,128)(2,1)} %param.13) | copy-start | bytes 3145732
  163.6 4.2 %copy-start.1 = (f32[2,2048,128]{2,1,0:T(8,128)S(1)}, f32[2,2048,128]{2,1,0:T(8,128)}, u32[]{:S(2)}) copy-start(f32[2,2048,128]{2,1,0:T(8,128)} %get-tuple-element.373) | copy-start | bytes 6291460 | tf_op jit(solution)/shard_map/while
  173.9 1.4 copy-start.2
  179.0 4.2 %copy-start.1 = (f32[2,2048,128]{2,1,0:T(8,128)S(1)}, f32[2,2048,128]{2,1,0:T(8,128)}, u32[]{:S(2)}) copy-start(f32[2,2048,128]{2,1,0:T(8,128)} %get-tuple-element.373) | copy-start | bytes 6291460 | tf_op jit(solution)/shard_map/while
  189.3 1.4 copy-start.2
  194.5 4.2 %copy-start.1 = (f32[2,2048,128]{2,1,0:T(8,128)S(1)}, f32[2,2048,128]{2,1,0:T(8,128)}, u32[]{:S(2)}) copy-start(f32[2,2048,128]{2,1,0:T(8,128)} %get-tuple-element.373) | copy-start | bytes 6291460 | tf_op jit(solution)/shard_map/while
  204.8 1.4 copy-start.2
  209.9 4.2 %copy-start.1 = (f32[2,2048,128]{2,1,0:T(8,128)S(1)}, f32[2,2048,128]{2,1,0:T(8,128)}, u32[]{:S(2)}) copy-start(f32[2,2048,128]{2,1,0:T(8,128)} %get-tuple-element.373) | copy-start | bytes 6291460 | tf_op jit(solution)/shard_map/while
  220.2 1.4 copy-start.2
where the time goes:
time: 269 us; the launch traced here: 268 us
  waiting for transfers between devices  113 us (42%)
  matrix products  59.8 us (22%)
  other arithmetic  39.9 us (15%)
  local copies, waits for them, and re-layouts  32.3 us (12%)
  starting transfers between devices  20.8 us (8%)
    all_to_all x1, waiting for transfers between devices, shards(): lax.all_to_all(kv_pool[lax.all_to_all(request_table, 'pool', split_axis=0...  88.6 us
    dot_general x6, matrix products, absorb(): jnp.einsum('hck,kd->hcd', weights.astype(jnp.bfloat16), value_rows, prefe...  39 us
    reduce_sum x6, other arithmetic, absorb(): running_sum = running_sum * correction + jnp.sum(weights, axis=2)  24.7 us
    dot_general x6, matrix products, absorb(): jnp.einsum('chd,kd->hck', query_rows, key_rows, preferred_element_type=jn...  20.8 us
    all_to_all x1, waiting for transfers between devices, shards(): lax.all_to_all(outgoing, 'pool', split_axis=0, concat_axis=0, tiled=True)  18.7 us
    unnamed x10, local copies, waits for them, and re-layouts  9.62 us
    all_to_all x1, starting transfers between devices, shards(): lax.all_to_all(dest_slots, 'pool', split_axis=0, concat_axis=0, tiled=True)  7.28 us
    all_to_all x1, starting transfers between devices, shards(): lax.all_to_all(request_table, 'pool', split_axis=0, concat_axis=0, tiled=...  5.41 us
  transfers between devices with their start and end apart: 4, of which 4 were waited for; matrix products, arithmetic and copies ran while one was open for 5% of the time, Pallas kernels for 0%

commit v1 on v0

v1 whole, which is shorter than its diff:
```python
import functools
import math

import jax
import jax.numpy as jnp
from jax import lax
from jax.experimental import pallas as pl
from jax.experimental.pallas import tpu as pltpu
from jax.sharding import PartitionSpec as P

masked_score = -1e30


def place_cells(owners, slot_ids, is_live, per_owner, pool_count):
    how_many = owners.shape[0]
    indices = jnp.arange(how_many, dtype=jnp.int32)
    earlier = indices[:, None] > indices[None, :]
    same_owner = owners[:, None] == owners[None, :]
    position = jnp.sum(jnp.where(earlier & same_owner & is_live[None, :], 1, 0), axis=1).astype(
        jnp.int32
    )
    cell_ids = jnp.where(is_live, owners * per_owner + position, -1)
    matches = cell_ids[:, None] == jnp.arange(pool_count * per_owner, dtype=jnp.int32)[None, :]
    slot_table = jnp.sum(jnp.where(matches, slot_ids[:, None], 0), axis=0)
    return (cell_ids, matches, slot_table.reshape(pool_count, per_owner))


def absorb(q, k, v, m, acc, scale, keep=None):
    s = lax.dot_general(q, k, (((1,), (1,)), ((), ())), preferred_element_type=jnp.float32)
    if keep is not None:
        s = jnp.where(keep, s, masked_score)
    top = jnp.max(s, axis=1, keepdims=True)
    new_m = jnp.maximum(m, top)
    p = jnp.exp2((s - new_m[:, :1]) * scale).astype(jnp.bfloat16)
    fade = jnp.exp2((m - new_m) * scale)[:, :1]
    acc = acc * fade + jnp.dot(p, v, preferred_element_type=jnp.float32)
    return new_m, acc


def attend_kernel(
    len_ref, q_ref, new_ref, prefix_ref, out_ref, key_ref, value_ref, *, scale, block, heads, page_len, slice_len
):
    parts, _, part_len, dim = prefix_ref.shape
    new_len = new_ref.shape[1]
    rows = q_ref.shape[0]
    tokens = rows // heads
    prefix_total = parts * part_len
    step = pl.program_id(0)

    @pl.when(step == 0)
    def _():
        first = prefix_ref[0, 0, 0:16, :].astype(jnp.float32)[0:1, :]
        index = lax.broadcasted_iota(jnp.int32, (part_len, dim), 0)
        for part in range(parts):
            place = index // slice_len * page_len + part * slice_len + index % slice_len
            live = place < len_ref[0]
            rows_here = pl.ds(part * part_len, part_len)
            keys = prefix_ref[part, 0].astype(jnp.float32)
            key_ref[rows_here, :] = jnp.where(live, keys, first).astype(jnp.bfloat16)
            values = prefix_ref[part, 1].astype(jnp.float32)
            value_ref[rows_here, 0:dim] = jnp.where(live, values, 0.0).astype(jnp.bfloat16)
            value_ref[rows_here, dim:] = jnp.where(live, 1.0, 0.0).astype(jnp.bfloat16)
        value_ref[prefix_total:, 0:dim] = new_ref[1]
        value_ref[prefix_total:, dim:] = jnp.ones((new_len, dim), jnp.bfloat16)

    q = q_ref[...]
    m = jnp.full((rows, dim), masked_score, jnp.float32)
    acc = jnp.zeros((rows, 2 * dim), jnp.float32)

    def new_block(at, carry, keep=None):
        start = pl.multiple_of(at * block, block)
        k = new_ref[0, pl.ds(start, block), :]
        v = value_ref[pl.ds(prefix_total + start, block), :]
        return absorb(q, k, v, *carry, scale, keep)

    full = step * tokens // block
    row_token = step * tokens + lax.broadcasted_iota(jnp.int32, (rows, block), 0) // heads
    key_token = full * block + lax.broadcasted_iota(jnp.int32, (rows, block), 1)
    carry = new_block(full, (m, acc), key_token <= row_token)
    carry = lax.fori_loop(0, full, new_block, carry)
    for part in range(parts):
        here = pl.ds(part * part_len, part_len)
        carry = absorb(q, key_ref[here, :], value_ref[here, :], *carry, scale)
    acc = carry[1]
    out_ref[...] = (acc[:, :dim] / acc[:, dim:]).astype(out_ref.dtype)


def attend(q, new_pairs, prefix, length, page_len, slice_len, heads):
    rows, dim = q.shape
    new_len = new_pairs.shape[1]
    row_block = math.gcd(rows, 512)
    block = math.gcd(new_len, 512)
    parts, _, part_len, _ = prefix.shape
    kernel = functools.partial(
        attend_kernel,
        scale=math.log2(math.e) / math.sqrt(dim),
        block=block,
        heads=heads,
        page_len=page_len,
        slice_len=slice_len,
    )
    return pl.pallas_call(
        kernel,
        out_shape=jax.ShapeDtypeStruct((rows, dim), jnp.bfloat16),
        grid=(rows // row_block,),
        in_specs=[
            pl.BlockSpec(memory_space=pltpu.SMEM),
            pl.BlockSpec((row_block, dim), lambda i: (i, 0)),
            pl.BlockSpec(new_pairs.shape, lambda i: (0, 0, 0)),
            pl.BlockSpec(prefix.shape, lambda i: (0, 0, 0, 0)),
        ],
        out_specs=pl.BlockSpec((row_block, dim), lambda i: (i, 0)),
        scratch_shapes=[
            pltpu.VMEM((parts * part_len, dim), jnp.bfloat16),
            pltpu.VMEM((parts * part_len + new_len, 2 * dim), jnp.bfloat16),
        ],
        compiler_params=pltpu.CompilerParams(vmem_limit_bytes=48 * 1024 * 1024),
    )(length, q, new_pairs, prefix)


def exchange(x):
    return lax.all_to_all(x, "pool", split_axis=0, concat_axis=0, tiled=True)


def shards(queries, new_pairs, kv_pool, page_owner, page_slot, prefix_len, fresh_owner, fresh_slot):
    pool_count = lax.axis_size("pool")
    head_count = lax.axis_size("head")
    me_head = lax.axis_index("head")
    page_len = kv_pool.shape[2]
    dim = kv_pool.shape[3]
    slice_len = page_len // head_count
    max_pages = page_owner.shape[1]
    bucket = 2 * ((max_pages + pool_count - 1) // pool_count)
    new_len = new_pairs.shape[2]
    new_count = new_len // page_len
    write_bound = (new_count + pool_count - 1) // pool_count
    fresh_total = pool_count * write_bound
    length = prefix_len[0]

    live_pages = (length + page_len - 1) // page_len
    is_live = jnp.arange(max_pages, dtype=jnp.int32) < live_pages
    prefix_cells, _, request_table = place_cells(
        page_owner[0], page_slot[0], is_live, bucket, pool_count
    )
    fresh_cells, fresh_matches, dest_table = place_cells(
        fresh_owner[0],
        fresh_slot[0],
        jnp.ones((new_count,), dtype=bool),
        write_bound,
        pool_count,
    )
    filled = jnp.any(fresh_matches, axis=0).reshape(pool_count, write_bound)
    dest_slots = jnp.where(filled, dest_table, fresh_total)
    source = jnp.sum(
        jnp.where(fresh_matches, jnp.arange(new_count, dtype=jnp.int32)[:, None], 0), axis=0
    )
    tables = exchange(jnp.concatenate([request_table, dest_slots], axis=1))
    wanted, arrived_slots = tables[:, :bucket], tables[:, bucket:]

    pool_slice = lax.dynamic_slice_in_dim(kv_pool, me_head * slice_len, slice_len, 2)
    fetched = exchange(pool_slice[wanted]).reshape(pool_count * bucket, 2, slice_len, dim)
    mine = jnp.take(fetched, jnp.maximum(prefix_cells, 0), axis=0)
    mine = mine.transpose(1, 0, 2, 3).reshape(2, max_pages * slice_len, dim)
    prefix = lax.all_gather(mine, "head")

    new_pages = new_pairs[0].reshape(2, new_count, page_len, dim)
    new_slice = lax.dynamic_slice_in_dim(new_pages, me_head * slice_len, slice_len, 2)
    outgoing = jnp.take(new_slice.transpose(1, 0, 2, 3), source, axis=0)
    arrived = exchange(outgoing.reshape(pool_count, write_bound, 2, slice_len, dim))
    arrived = arrived.reshape(-1, 2, slice_len, dim)
    own = jnp.zeros((fresh_total, 2, slice_len, dim), jnp.bfloat16)
    own = own.at[arrived_slots.reshape(-1)].set(arrived, mode="drop")
    stored = lax.all_gather(own, "head")
    stored = stored.transpose(1, 2, 0, 3, 4).reshape(fresh_total, 2, page_len, dim)

    heads = queries.shape[2]
    attended = attend(
        queries.reshape(-1, dim), new_pairs[0], prefix, prefix_len, page_len, slice_len, heads
    )
    return (attended.reshape(queries.shape), stored)


def solution(mesh):
    in_specs = (
        P("pool", None, "head", None),
        P("pool", None, None, None),
        P("pool", None, None, None),
        P("pool", None),
        P("pool", None),
        P("pool"),
        P("pool", None),
        P("pool", None),
    )
    out_specs = (P("pool", None, "head", None), P("pool", None, None, None))
    return jax.shard_map(shards, mesh=mesh, in_specs=in_specs, out_specs=out_specs, check_vma=False)
```

time: 269 us -> 145 us (0.54)
  the two profiles are of different devices: /device:TPU:0 before, /device:TPU:28 now
where the time goes in v1:
time: 145 us; the launch traced here: 142 us
  Pallas kernels  44.2 us (30%)
  waiting for transfers between devices  40.9 us (28%)
  starting transfers between devices  19.8 us (14%)
  local copies, waits for them, and re-layouts  15 us (10%)
  between operations  14.8 us (10%)
  other arithmetic  7.47 us (5%)
    pallas_call x1, Pallas kernels, attend(): pl.pallas_call(kernel, out_shape=jax.ShapeDtypeStruct((rows, dim), jnp.bf...  44.2 us
    all_gather x1, waiting for transfers between devices, shards(): prefix = lax.all_gather(mine, 'head')  21.1 us
    all_to_all x3, starting transfers between devices, exchange(): return lax.all_to_all(x, 'pool', split_axis=0, concat_axis=0, tiled=True)  19.7 us
    all_to_all x3, waiting for transfers between devices, exchange(): return lax.all_to_all(x, 'pool', split_axis=0, concat_axis=0, tiled=True)  19.7 us
  transfers between devices with their start and end apart: 5, of which 3 were waited for; matrix products, arithmetic and copies ran while one was open for 10% of the time, Pallas kernels for 0%

profile of v1, /device:TPU:28, one launch (start us, length us, event | category | flops | bytes accessed | tf_op | source)
XLA Modules:
  0.0 142.2 jit_solution(3357661968955965965)
XLA Ops:
  7.8 0.9 select_reduce_fusion.1
  8.8 0.7 maximum_compare_fusion
  9.4 0.7 select_reduce_fusion
  10.2 0.1 reshape.147
  10.3 0.9 select_reduce_fusion.4
  11.2 0.7 multiply_add_fusion
  11.8 0.1 fusion.2
  11.9 0.7 select_reduce_fusion.2
  12.7 0.1 select_n.109
  12.8 0.7 pad_add_fusion
  13.5 6.0 %all-to-all-start = ((s32[8,1,20]{2,1,0:T(1,128)}), s32[8,1,20]{2,1,0:T(1,128)S(1)}, u32[]{:S(2)}, u32[]{:S(2)}) async-start(s32[8,1,20]{2,1,0:T(1,128)} %bitcast.8), calls=%async_computation | async-start | bytes 8192 | tf_op jit(solution)/shard_map/all_to_all | solution.py:122
  19.5 0.1 reduce_sum.57
  19.6 1.0 dynamic-slice_bitcast_fusion
  20.5 0.6 gather_fusion.2
  21.2 0.8 broadcast_select_fusion
  22.0 7.2 %all-to-all-start.2 = ((bf16[8,4,2,16,128]{4,3,2,1,0:T(8,128)(2,1)}), bf16[8,4,2,16,128]{4,3,2,1,0:T(8,128)(2,1)S(1)}, u32[]{:S(2)}, u32[]{:S(2)}) async-start(bf16[8,4,2,16,128]{4,3,2,1,0:T(8,128)(2,1)} %broadcast_select_fusion), calls=%async_computation.2 | async-start | bytes 524288 | tf_op jit(solution)/shard_map/all_to_all | solution.py:122
  29.2 1.4 constant_dynamic-slice_fusion
  30.6 0.1 reshape.155
  30.7 1.7 %gather_fusion = bf16[128,2,16,128]{3,2,1,0:T(8,128)(2,1)} fusion(bf16[128,2,16,128]{3,2,1,0:T(8,128)(2,1)S(1)} %constant_dynamic-slice_fusion, s32[1024]{0:T(1024)S(1)} %pad_clamp_fusion.2), kind=kCustom, calls=%fused_computation | custom fusion | bytes 2097664 | tf_op jit(solution)/shard_map/gather | solution.py:161
  32.3 2.2 %all-to-all-done.2 = bf16[8,4,2,16,128]{4,3,2,1,0:T(8,128)(2,1)S(1)} async-done(((bf16[8,4,2,16,128]{4,3,2,1,0:T(8,128)(2,1)}), bf16[8,4,2,16,128]{4,3,2,1,0:T(8,128)(2,1)S(1)}, u32[]{:S(2)}, u32[]{:S(2)}) %all-to-all-start.2) | async-done | bytes 262176 | tf_op jit(solution)/shard_map/all_to_all | solution.py:122
  34.5 6.5 %all-to-all-start.1 = ((bf16[8,16,2,16,128]{4,3,2,1,0:T(8,128)(2,1)}), bf16[8,16,2,16,128]{4,3,2,1,0:T(8,128)(2,1)S(1)}, u32[]{:S(2)}, u32[]{:S(2)}) async-start(bf16[8,16,2,16,128]{4,3,2,1,0:T(8,128)(2,1)} %bitcast.10), calls=%async_computation.1 | async-start | bytes 2097152 | tf_op jit(solution)/shard_map/all_to_all | solution.py:122
  41.1 0.1 reshape.150
  41.3 2.8 %scatter_fusion = bf16[32,2,16,128]{3,2,1,0:T(8,128)(2,1)S(1)} fusion(bf16[32,2,16,128]{3,2,1,0:T(8,128)(2,1)S(1)} %broadcast_in_dim.113, s32[32]{0:T(128)S(1)} %fusion.5, bf16[32,2,16,128]{3,2,1,0:T(8,128)(2,1)} %bitcast.55), kind=kCustom, calls=%fused_computation.3 | custom fusion | bytes 786560 | tf_op jit(solution)/shard_map/scatter | solution.py:172
  44.1 0.7 copy-done.3
  45.0 17.5 %all-to-all-done.1 = bf16[8,16,2,16,128]{4,3,2,1,0:T(8,128)(2,1)S(1)} async-done(((bf16[8,16,2,16,128]{4,3,2,1,0:T(8,128)(2,1)}), bf16[8,16,2,16,128]{4,3,2,1,0:T(8,128)(2,1)S(1)}, u32[]{:S(2)}, u32[]{:S(2)}) %all-to-all-start.1) | async-done | bytes 1048608 | tf_op jit(solution)/shard_map/all_to_all | solution.py:122
  62.5 1.4 gather_fusion.1
  63.9 1.2 select_bitcast_fusion
  65.1 0.8 copy.19
  66.0 2.5 %copy.20 = bf16[32,2,4,16,128]{4,3,2,1,0:T(8,128)(2,1)} copy(bf16[32,2,4,16,128]{4,3,1,0,2:T(8,128)(2,1)} %bitcast.53) | data formatting | bytes 2097152 | tf_op jit(solution)/shard_map/transpose | solution.py:174
  68.5 21.1 %all-gather.4.cloned.1.call-done.prefix_ref = bf16[4,2,1024,128]{3,2,1,0:T(8,128)(2,1)} async-done(((bf16[1,2,1024,128]{3,2,1,0:T(8,128)(2,1)}), bf16[4,2,1024,128]{3,2,1,0:T(8,128)(2,1)}) %all-gather.4.cloned.1.call-update) | async-done | bytes 2097168 | tf_op jit(solution)/shard_map/all_gather | solution.py:164
  89.6 1.6 %copy-done = bf16[4,2,1024,128]{3,2,1,0:T(8,128)(2,1)S(1)} copy-done((bf16[4,2,1024,128]{3,2,1,0:T(8,128)(2,1)S(1)}, bf16[4,2,1024,128]{3,2,1,0:T(8,128)(2,1)}, u32[]{:S(2)}) %copy-start) | copy-done | bytes 2097176
  91.2 44.2 %shard_map.95 = bf16[4096,128]{1,0:T(8,128)(2,1)} custom-call(s32[1]{0:T(128)S(6)} %copy.22.len_ref, bf16[4096,128]{1,0:T(8,128)(2,1)S(1)} %bitcast.49, bf16[2,2048,128]{2,1,0:T(8,128)(2,1)S(1)} %bitcast.48, bf16[4,2,1024,128]{3,2,1,0:T(8,128)(2,1)S(1)} %copy-done), custom_call_target="tpu_custom_call" | custom-call | tf_op jit(solution)/shard_map/pallas_call | solution.py:102
  (28 shorter events, 0.3 us)
Async XLA Ops:
  13.5 8.5 %all-to-all-start = ((s32[8,1,20]{2,1,0:T(1,128)}), s32[8,1,20]{2,1,0:T(1,128)S(1)}, u32[]{:S(2)}, u32[]{:S(2)}) async-start(s32[8,1,20]{2,1,0:T(1,128)} %bitcast.8), calls=%async_computation | async-start | bytes 8192 | tf_op jit(solution)/shard_map/all_to_all | solution.py:122
  22.0 22.9 %copy-start.5 = (s32[1,64]{1,0:T(1,128)S(1)}, s32[1,64]{1,0:T(1,128)}, u32[]{:S(2)}) copy-start(s32[1,64]{1,0:T(1,128)} %param.11) | copy-start | bytes 772
  22.0 12.5 %all-to-all-start.2 = ((bf16[8,4,2,16,128]{4,3,2,1,0:T(8,128)(2,1)}), bf16[8,4,2,16,128]{4,3,2,1,0:T(8,128)(2,1)S(1)}, u32[]{:S(2)}, u32[]{:S(2)}) async-start(bf16[8,4,2,16,128]{4,3,2,1,0:T(8,128)(2,1)} %broadcast_select_fusion), calls=%async_computation.2 | async-start | bytes 524288 | tf_op jit(solution)/shard_map/all_to_all | solution.py:122
  34.5 6.7 %copy-start.4 = (bf16[8,4,2,16,128]{4,3,2,1,0:T(8,128)(2,1)}, bf16[8,4,2,16,128]{4,3,2,1,0:T(8,128)(2,1)S(1)}, u32[]{:S(2)}) copy-start(bf16[8,4,2,16,128]{4,3,2,1,0:T(8,128)(2,1)S(1)} %all-to-all-done.2) | copy-start | bytes 786436
  34.5 55.1 %copy-start.1 = (bf16[1,2,2048,128]{3,2,1,0:T(8,128)(2,1)S(1)}, bf16[1,2,2048,128]{3,2,1,0:T(8,128)(2,1)}, u32[]{:S(2)}) copy-start(bf16[1,2,2048,128]{3,2,1,0:T(8,128)(2,1)} %param.9) | copy-start | bytes 3145732
  34.5 55.1 %copy-start.2 = (bf16[1,2048,2,128]{3,2,1,0:T(2,128)(2,1)S(1)}, bf16[1,2048,2,128]{3,2,1,0:T(2,128)(2,1)}, u32[]{:S(2)}) copy-start(bf16[1,2048,2,128]{3,2,1,0:T(2,128)(2,1)} %param.8) | copy-start | bytes 3145732
  34.5 28.0 %all-to-all-start.1 = ((bf16[8,16,2,16,128]{4,3,2,1,0:T(8,128)(2,1)}), bf16[8,16,2,16,128]{4,3,2,1,0:T(8,128)(2,1)S(1)}, u32[]{:S(2)}, u32[]{:S(2)}) async-start(bf16[8,16,2,16,128]{4,3,2,1,0:T(8,128)(2,1)} %bitcast.10), calls=%async_computation.1 | async-start | bytes 2097152 | tf_op jit(solution)/shard_map/all_to_all | solution.py:122
  41.1 24.9 %all-gather.6.cloned.1.call-start = ((), (), s32[]{:S(2)}) async-start(), calls=%async_computation.4 | async-start | bytes 1310720 | tf_op jit(solution)/shard_map/all_gather | solution.py:173
  44.1 0.7 copy-start.3
  44.9 44.7 %all-gather.4.cloned.1.call-start = ((), (), s32[]{:S(2)}) async-start(), calls=%async_computation.3 | async-start | bytes 2621440 | tf_op jit(solution)/shard_map/all_gather | solution.py:164
  89.6 1.6 %copy-start = (bf16[4,2,1024,128]{3,2,1,0:T(8,128)(2,1)S(1)}, bf16[4,2,1024,128]{3,2,1,0:T(8,128)(2,1)}, u32[]{:S(2)}) copy-start(bf16[4,2,1024,128]{3,2,1,0:T(8,128)(2,1)} %all-gather.4.cloned.1.call-done.prefix_ref) | copy-start | bytes 6291460
Sparse Core Ops, SparseCore 0:
  45.0 17.6 all-gather.5
  66.0 23.5 all-gather.3

commit v2 on v1

v2 whole, which is shorter than its diff:
```python
import functools
import math

import jax
import jax.numpy as jnp
from jax import lax
from jax.experimental import pallas as pl
from jax.experimental.pallas import tpu as pltpu
from jax.sharding import PartitionSpec as P

masked_score = -1e30
MESH = pl.DeviceIdType.MESH


def place_cells(owners, slot_ids, is_live, per_owner, pool_count):
    how_many = owners.shape[0]
    indices = jnp.arange(how_many, dtype=jnp.int32)
    earlier = indices[:, None] > indices[None, :]
    same_owner = owners[:, None] == owners[None, :]
    position = jnp.sum(jnp.where(earlier & same_owner & is_live[None, :], 1, 0), axis=1).astype(
        jnp.int32
    )
    cell_ids = jnp.where(is_live, owners * per_owner + position, -1)
    matches = cell_ids[:, None] == jnp.arange(pool_count * per_owner, dtype=jnp.int32)[None, :]
    slot_table = jnp.sum(jnp.where(matches, slot_ids[:, None], 0), axis=0)
    return (cell_ids, matches, slot_table.reshape(pool_count, per_owner))


def absorb(q, k, v, m, acc, scale, keep=None):
    s = lax.dot_general(q, k, (((1,), (1,)), ((), ())), preferred_element_type=jnp.float32)
    if keep is not None:
        s = jnp.where(keep, s, masked_score)
    top = jnp.max(s, axis=1, keepdims=True)
    new_m = jnp.maximum(m, top)
    p = jnp.exp2((s - new_m[:, :1]) * scale).astype(jnp.bfloat16)
    fade = jnp.exp2((m - new_m) * scale)[:, :1]
    acc = acc * fade + jnp.dot(p, v, preferred_element_type=jnp.float32)
    return new_m, acc


def fused_kernel(
    len_ref,
    cell_ref,
    source_ref,
    table_ref,
    q_ref,
    new_ref,
    pool_ref,
    out_ref,
    stored_ref,
    slice_ref,
    asked_ref,
    asked_smem,
    place_ref,
    place_smem,
    page_out,
    key_in,
    value_in,
    fresh_out,
    fresh_in,
    part_ref,
    value_ref,
    new_value_ref,
    m_ref,
    acc_ref,
    load_sem,
    small_sem,
    table_send,
    table_recv,
    fresh_send,
    fresh_recv,
    page_send,
    page_recv,
    part_send,
    part_recv,
    stored_send,
    stored_recv,
    *,
    scale,
    row_block,
    heads,
):
    pools, _, bucket, piece, dim = page_out.shape[1], 2, page_out.shape[2], page_out.shape[3], page_out.shape[4]
    head_count = part_ref.shape[0]
    part_len = part_ref.shape[2]
    bound = fresh_out.shape[1]
    slots = stored_ref.shape[0]
    page_len = stored_ref.shape[2]
    max_pages = cell_ref.shape[0]
    new_pages = new_ref.shape[1]
    page_in = (key_in, value_in)
    me = lax.axis_index("pool")
    side = lax.axis_index("head")
    mine = pl.ds(pl.multiple_of(side * piece, piece), piece)
    by_pair = side + 1 - 2 * (side % 2)
    half = head_count // 2
    across = (side + half) % head_count

    load = pltpu.make_async_copy(pool_ref.at[:, :, mine, :], slice_ref, load_sem)
    load.start()

    barrier = pltpu.get_barrier_semaphore()

    def greet(d, carry):
        pl.semaphore_signal(barrier, inc=1, device_id={"pool": (me + d) % pools}, device_id_type=MESH)
        return carry

    lax.fori_loop(1, pools, greet, 0)
    for peer in (by_pair, across):
        pl.semaphore_signal(barrier, inc=1, device_id={"head": peer}, device_id_type=MESH)
    pl.semaphore_wait(barrier, pools - 1 + 2)

    def remote(src, dst, send, recv, axis, peer):
        return pltpu.make_async_remote_copy(
            src_ref=src,
            dst_ref=dst,
            send_sem=send,
            recv_sem=recv,
            device_id={axis: peer},
            device_id_type=MESH,
        )

    def table_copy(d):
        to = (me + d) % pools
        return remote(table_ref.at[to], asked_ref.at[me], table_send.at[d], table_recv.at[d], "pool", to)

    def fresh_copy(d):
        to = (me + d) % pools
        return remote(fresh_out.at[to], fresh_in.at[me], fresh_send.at[d], fresh_recv.at[d], "pool", to)

    def page_copy(kv, d):
        to = (me + d) % pools
        return remote(
            page_out.at[kv, to], page_in[kv].at[me], page_send.at[kv, d], page_recv.at[kv, d], "pool", to
        )

    def each(start, stop, act):
        def body(d, carry):
            act(d)
            return carry

        lax.fori_loop(start, stop, body, 0)

    each(1, pools, lambda d: table_copy(d).start())
    asked_ref[me] = table_ref[me]
    load.wait()
    each(1, pools, lambda d: table_copy(d).wait())
    total = asked_ref[0, 1:2, :]
    for r in range(1, pools):
        total = total + asked_ref[r, 1:2, :]
    place_ref[...] = total
    to_smem = pltpu.make_async_copy(asked_ref, asked_smem, small_sem.at[0])
    to_smem.start()
    place_copy = pltpu.make_async_copy(place_ref, place_smem, small_sem.at[1])
    place_copy.start()
    to_smem.wait()
    place_copy.wait()

    def pages_to(kv, d):
        to = (me + d) % pools
        for c in range(bucket):
            page_out[kv, to, c] = slice_ref[asked_smem[to, 0, c], kv]

    for kv in range(2):

        def send_pages(d):
            pages_to(kv, d)
            page_copy(kv, d).start()

        each(1, pools, send_pages)
        pages_to(kv, 0)
        page_in[kv][me] = page_out[kv, me]

    def fresh_to(d):
        to = (me + d) % pools
        for c in range(bound):
            page = source_ref[to * bound + c]
            for kv in range(2):
                fresh_out[to, c, kv] = new_ref[kv, page, mine, :]

    def send_fresh(d):
        fresh_to(d)
        fresh_copy(d).start()

    each(1, pools, send_fresh)
    fresh_to(0)
    fresh_in[me] = fresh_out[me]

    new_value_ref[:, 0:dim] = new_ref[1].reshape(new_pages * page_len, dim)
    new_value_ref[:, dim:] = jnp.ones((new_pages * page_len, dim), jnp.bfloat16)
    tokens = row_block // heads
    row_blocks = q_ref.shape[0] // row_block

    def new_rows(i):
        rows = pl.ds(pl.multiple_of(i * row_block, row_block), row_block)
        q = q_ref[rows, :]
        m = jnp.full((row_block, dim), masked_score, jnp.float32)
        acc = jnp.zeros((row_block, 2 * dim), jnp.float32)

        def new_block(at, carry, keep=None):
            k = new_ref[0, pl.ds(at * (tokens // page_len), tokens // page_len)].reshape(tokens, dim)
            v = new_value_ref[pl.ds(pl.multiple_of(at * tokens, tokens), tokens), :]
            return absorb(q, k, v, *carry, scale, keep)

        row_token = lax.broadcasted_iota(jnp.int32, (row_block, tokens), 0) // heads
        keep = lax.broadcasted_iota(jnp.int32, (row_block, tokens), 1) <= row_token
        m, acc = lax.fori_loop(0, i, new_block, new_block(i, (m, acc), keep))
        m_ref[rows, :] = m
        acc_ref[rows, :] = acc

    def part_copy(kv, which):
        part, peer = ((side, across), (side, by_pair), (across, by_pair))[which]
        return remote(
            part_ref.at[part, kv],
            part_ref.at[part, kv],
            part_send.at[kv, which],
            part_recv.at[kv, which],
            "head",
            peer,
        )

    def collect(kv):
        each(1, pools, lambda d: page_copy(kv, d).wait())

        def four(g, carry):
            for j in range(4):
                cell = cell_ref[g * 4 + j]
                rows = pl.ds(pl.multiple_of((g * 4 + j) * piece, piece), piece)
                part_ref[side, kv, rows, :] = page_in[kv][cell // bucket, cell % bucket]
            return carry

        lax.fori_loop(0, max_pages // 4, four, 0)
        part_copy(kv, 0).start()
        part_copy(kv, 1).start()

    each(0, row_blocks * 5 // 8, new_rows)
    collect(0)
    each(row_blocks * 5 // 8, row_blocks, new_rows)
    part_copy(0, 0).wait()
    part_copy(0, 2).start()
    collect(1)

    each(1, pools, lambda d: fresh_copy(d).wait())

    def keep_page(s):
        at = place_smem[0, s]
        cell = jnp.maximum(at - 1, 0)
        filled = jnp.full((piece, dim), at, jnp.int32) > 0
        for kv in range(2):
            page = fresh_in[cell // bound, cell % bound, kv].astype(jnp.float32)
            stored_ref[s, kv, mine, :] = jnp.where(filled, page, 0.0).astype(jnp.bfloat16)

    each(0, slots, keep_page)

    def stored_copy(which):
        part, peer = ((side, across), (side, by_pair), (across, by_pair))[which]
        rows = stored_ref.at[:, :, pl.ds(pl.multiple_of(part * piece, piece), piece), :]
        return remote(rows, rows, stored_send.at[which], stored_recv.at[which], "head", peer)

    stored_copy(0).start()
    stored_copy(1).start()
    part_copy(1, 0).wait()
    part_copy(1, 2).start()
    stored_copy(0).wait()
    stored_copy(2).start()
    for which in (1, 2):
        part_copy(0, which).wait()
        part_copy(1, which).wait()

    def stored_wait():
        stored_copy(1).wait()
        stored_copy(2).wait()

    first = part_ref[0, 0, 0:16, :].astype(jnp.float32)[0:1, :]
    index = lax.broadcasted_iota(jnp.int32, (part_len, dim), 0)
    for part in range(head_count):
        place = index // piece * page_len + part * piece + index % piece
        live = place < len_ref[0]
        keys = part_ref[part, 0].astype(jnp.float32)
        part_ref[part, 0] = jnp.where(live, keys, first).astype(jnp.bfloat16)
        values = part_ref[part, 1].astype(jnp.float32)
        value_ref[part, :, 0:dim] = jnp.where(live, values, 0.0).astype(jnp.bfloat16)
        value_ref[part, :, dim:] = jnp.where(live, 1.0, 0.0).astype(jnp.bfloat16)

    def prefix_rows(i):
        rows = pl.ds(pl.multiple_of(i * row_block, row_block), row_block)
        q = q_ref[rows, :]
        carry = (m_ref[rows, :], acc_ref[rows, :])
        for part in range(head_count):
            carry = absorb(q, part_ref[part, 0], value_ref[part], *carry, scale)
        acc = carry[1]
        out_ref[rows, :] = (acc[:, :dim] / acc[:, dim:]).astype(out_ref.dtype)

    each(0, row_blocks, prefix_rows)
    stored_wait()


def fused(q, new_pairs, kv_pool, table, cells, source, length, slots, bucket, bound, pools, head_count, heads):
    rows, dim = q.shape
    new_pages, page_len = new_pairs.shape[1:3]
    piece = page_len // head_count
    max_pages = cells.shape[0]
    row_block = math.gcd(rows, 512)
    kernel = functools.partial(
        fused_kernel,
        scale=math.log2(math.e) / math.sqrt(dim),
        row_block=row_block,
        heads=heads,
    )
    bf16, dma = jnp.bfloat16, pltpu.SemaphoreType.DMA
    smem, vmem = pl.BlockSpec(memory_space=pltpu.SMEM), pl.BlockSpec(memory_space=pltpu.VMEM)
    part_len = max_pages * piece
    return pl.pallas_call(
        kernel,
        out_shape=(
            jax.ShapeDtypeStruct((rows, dim), bf16),
            jax.ShapeDtypeStruct((slots, 2, page_len, dim), bf16),
        ),
        in_specs=[smem, smem, smem, vmem, vmem, vmem, pl.BlockSpec(memory_space=pl.ANY)],
        out_specs=(vmem, vmem),
        scratch_shapes=[
            pltpu.VMEM((kv_pool.shape[0], 2, piece, dim), bf16),
            pltpu.VMEM(table.shape, jnp.int32),
            pltpu.SMEM(table.shape, jnp.int32),
            pltpu.VMEM((1, 128), jnp.int32),
            pltpu.SMEM((1, 128), jnp.int32),
            pltpu.VMEM((2, pools, bucket, piece, dim), bf16),
            pltpu.VMEM((pools, bucket, piece, dim), bf16),
            pltpu.VMEM((pools, bucket, piece, dim), bf16),
            pltpu.VMEM((pools, bound, 2, piece, dim), bf16),
            pltpu.VMEM((pools, bound, 2, piece, dim), bf16),
            pltpu.VMEM((head_count, 2, part_len, dim), bf16),
            pltpu.VMEM((head_count, part_len, 2 * dim), bf16),
            pltpu.VMEM((new_pages * page_len, 2 * dim), bf16),
            pltpu.VMEM((rows, dim), jnp.float32),
            pltpu.VMEM((rows, 2 * dim), jnp.float32),
            dma,
            dma((2,)),
            dma((pools,)),
            dma((pools,)),
            dma((pools,)),
            dma((pools,)),
            dma((2, pools)),
            dma((2, pools)),
            dma((2, 3)),
            dma((2, 3)),
            dma((3,)),
            dma((3,)),
        ],
        compiler_params=pltpu.CompilerParams(
            vmem_limit_bytes=56 * 1024 * 1024, collective_id=0, has_side_effects=True
        ),
    )(length, cells, source, table, q, new_pairs, kv_pool)


def shards(queries, new_pairs, kv_pool, page_owner, page_slot, prefix_len, fresh_owner, fresh_slot):
    pool_count = lax.axis_size("pool")
    head_count = lax.axis_size("head")
    page_len = kv_pool.shape[2]
    dim = kv_pool.shape[3]
    max_pages = page_owner.shape[1]
    bucket = 2 * ((max_pages + pool_count - 1) // pool_count)
    new_len = new_pairs.shape[2]
    new_count = new_len // page_len
    write_bound = (new_count + pool_count - 1) // pool_count
    fresh_total = pool_count * write_bound
    length = prefix_len[0]

    live_pages = (length + page_len - 1) // page_len
    is_live = jnp.arange(max_pages, dtype=jnp.int32) < live_pages
    prefix_cells, _, request_table = place_cells(
        page_owner[0], page_slot[0], is_live, bucket, pool_count
    )
    fresh_cells, fresh_matches, _ = place_cells(
        fresh_owner[0],
        fresh_slot[0],
        jnp.ones((new_count,), dtype=bool),
        write_bound,
        pool_count,
    )
    source = jnp.sum(
        jnp.where(fresh_matches, jnp.arange(new_count, dtype=jnp.int32)[:, None], 0), axis=0
    )
    rank = fresh_cells % write_bound + lax.axis_index("pool") * write_bound + 1
    spot = fresh_owner[0] * 128 + fresh_slot[0]
    lanes = jnp.arange(pool_count * 128, dtype=jnp.int32)
    places = jnp.sum(jnp.where(spot[:, None] == lanes[None, :], rank[:, None], 0), axis=0)
    table = jnp.stack(
        [jnp.pad(request_table, ((0, 0), (0, 128 - bucket))), places.reshape(pool_count, 128)], axis=1
    )

    heads = queries.shape[2]
    attended, stored = fused(
        queries.reshape(-1, dim),
        new_pairs[0].reshape(2, new_count, page_len, dim),
        kv_pool,
        table,
        jnp.maximum(prefix_cells, 0),
        source,
        prefix_len,
        fresh_total,
        bucket,
        write_bound,
        pool_count,
        head_count,
        heads,
    )
    return (attended.reshape(queries.shape), stored)


def solution(mesh):
    in_specs = (
        P("pool", None, "head", None),
        P("pool", None, None, None),
        P("pool", None, None, None),
        P("pool", None),
        P("pool", None),
        P("pool"),
        P("pool", None),
        P("pool", None),
    )
    out_specs = (P("pool", None, "head", None), P("pool", None, None, None))
    return jax.shard_map(shards, mesh=mesh, in_specs=in_specs, out_specs=out_specs, check_vma=False)
```

time: 145 us -> 97.5 us (0.67); the launches traced: 142 us -> 97.2 us
  Pallas kernels: 44.2 us -> 85.2 us
  waiting for transfers between devices: 40.9 us -> 0 us
  starting transfers between devices: 19.8 us -> 0 us
  between operations: 14.8 us -> 1.33 us
  local copies, waits for them, and re-layouts: 15 us -> 4.96 us
  other arithmetic: 7.47 us -> 5.75 us
    pallas_call x1, Pallas kernels: 44.2 us -> 85.2 us  [fused(): pl.pallas_call(kernel, out_shape=(jax.ShapeDtypeStruct((rows, dim), bf16)...]
    all_gather x2 -> x0, waiting for transfers between devices: 21.2 us -> none  [the longest x1 21.1 us: shards(): prefix = lax.all_gather(mine, 'head')]
    all_to_all x3 -> x0, starting transfers between devices: 19.7 us -> none  [exchange(): return lax.all_to_all(x, 'pool', split_axis=0, concat_axis=0, tiled=True)]
    all_to_all x3 -> x0, waiting for transfers between devices: 19.7 us -> none  [exchange(): return lax.all_to_all(x, 'pool', split_axis=0, concat_axis=0, tiled=True)]
    gather x3 -> x0, local copies, waits for them, and re-layouts: 3.69 us -> none  [the longest x1 1.66 us: shards(): pool_slice[wanted]]
    transpose x2 -> x0, local copies, waits for them, and re-layouts: 3.49 us -> none  [the longest x1 2.5 us: shards(): stored.transpose(1, 2, 0, 3, 4).reshape(fresh_total, 2, page_len, dim)]
    scatter x1 -> x0, local copies, waits for them, and re-layouts: 2.84 us -> none  [shards(): own = own.at[arrived_slots.reshape(-1)].set(arrived, mode='drop')]
    unnamed x12 -> x2, local copies, waits for them, and re-layouts: 2.32 us -> 4.88 us
  transfers between devices with their start and end apart: 5 -> 0, of which waited for: 3 -> 0; matrix products, arithmetic and copies ran while one was open for 10% -> 0% of each run, Pallas kernels for 0% -> 0%
where the time goes in v2:
time: 97.5 us; the launch traced here: 97.2 us
  Pallas kernels  85.2 us (87%)
  other arithmetic  5.75 us (6%)
  local copies, waits for them, and re-layouts  4.96 us (5%)
  between operations  1.33 us (1%)
    pallas_call x1, Pallas kernels, fused(): pl.pallas_call(kernel, out_shape=(jax.ShapeDtypeStruct((rows, dim), bf16)...  85.2 us
    unnamed x2, local copies, waits for them, and re-layouts  4.88 us

profile of v2, /device:TPU:28, one launch (start us, length us, event | category | flops | bytes accessed | tf_op | source)
XLA Modules:
  0.0 97.2 jit_solution(9652172806649793540)
XLA Ops:
  1.3 0.9 select_reduce_fusion.4
  2.2 0.9 select_reduce_fusion.2
  3.1 1.2 %broadcast_maximum_fusion = (s32[64]{0:T(128)}, s32[64]{0:T(128)S(1)}) fusion(s32[64]{0:T(128)S(1)} %select_reduce_fusion.2, s32[1,64]{1,0:T(1,128)} %param.11, s32[]{:T(128)S(6)} %select_n.45), kind=kLoop, calls=%fused_computation.24 | loop fusion | flops 320 | bytes 1028 | tf_op jit(solution)/shard_map/max | solution.py:398
  4.3 0.7 select_reduce_fusion.1
  5.1 0.7 fusion.4
  5.8 0.6 select_reduce_fusion.3.source_ref
  6.4 0.1 select_reduce_fusion
  6.5 0.1 reshape.71
  6.5 0.6 pad_add_fusion.table_ref
  7.2 85.2 %shard_map.95 = (bf16[4096,128]{1,0:T(8,128)(2,1)}, bf16[32,2,64,128]{3,2,1,0:T(8,128)(2,1)}) custom-call(s32[1]{0:T(128)S(6)} %copy.12.len_ref, s32[64]{0:T(128)} %get-tuple-element.8.cell_ref, s32[32]{0:T(128)} %select_reduce_fusion.3.source_ref, s32[8,2,128]{2,1,0:T(2,128)} %pad_add_fusion.table_ref, bf16[4096,128]{1,0:T(8,128)(2,1)} %bitcast.17, ...), custom_call_target="tpu_custom_call" | custom-call | tf_op jit(solution)/shard_map/pallas_call | solution.py:313
  92.3 2.6 %copy.13 = bf16[1,2048,2,128]{3,2,1,0:T(2,128)(2,1)} copy(bf16[1,2048,2,128]{3,2,1,0:T(2,128)(2,1)} %bitcast.16) | data formatting | bytes 2097152
  94.9 2.3 %copy.14 = bf16[32,2,64,128]{3,2,1,0:T(8,128)(2,1)} copy(bf16[32,2,64,128]{3,2,1,0:T(8,128)(2,1)} %get-tuple-element.14) | data formatting | bytes 2097152
  (2 shorter events, 0.0 us)

commit v3 on v2

--- a/solution.py
+++ b/solution.py
@@ -30,6 +30,10 @@
     s = lax.dot_general(q, k, (((1,), (1,)), ((), ())), preferred_element_type=jnp.float32)
     if keep is not None:
         s = jnp.where(keep, s, masked_score)
+    return weigh(s, v, m, acc, scale)
+
+
+def weigh(s, v, m, acc, scale):
     top = jnp.max(s, axis=1, keepdims=True)
     new_m = jnp.maximum(m, top)
     p = jnp.exp2((s - new_m[:, :1]) * scale).astype(jnp.bfloat16)
@@ -54,8 +58,8 @@
     place_ref,
     place_smem,
     page_out,
-    key_in,
-    value_in,
+    first_in,
+    second_in,
     fresh_out,
     fresh_in,
     part_ref,
@@ -80,15 +84,15 @@
     row_block,
     heads,
 ):
-    pools, _, bucket, piece, dim = page_out.shape[1], 2, page_out.shape[2], page_out.shape[3], page_out.shape[4]
-    head_count = part_ref.shape[0]
-    part_len = part_ref.shape[2]
+    _, pools, bucket, _, piece, dim = page_out.shape
+    part_len = cell_ref.shape[0] // 2 * piece
+    head_count = part_ref.shape[2] // part_len
     bound = fresh_out.shape[1]
     slots = stored_ref.shape[0]
     page_len = stored_ref.shape[2]
     max_pages = cell_ref.shape[0]
     new_pages = new_ref.shape[1]
-    page_in = (key_in, value_in)
+    page_in = (first_in, second_in)
     me = lax.axis_index("pool")
     side = lax.axis_index("head")
     mine = pl.ds(pl.multiple_of(side * piece, piece), piece)
@@ -156,20 +160,20 @@
     to_smem.wait()
     place_copy.wait()
 
-    def pages_to(kv, d):
+    def pages_to(part, d):
         to = (me + d) % pools
         for c in range(bucket):
-            page_out[kv, to, c] = slice_ref[asked_smem[to, 0, c], kv]
-
-    for kv in range(2):
+            page_out[part, to, c] = slice_ref[asked_smem[to, 0, part * bucket + c]]
+
+    for part in range(2):
 
         def send_pages(d):
-            pages_to(kv, d)
-            page_copy(kv, d).start()
+            pages_to(part, d)
+            page_copy(part, d).start()
 
         each(1, pools, send_pages)
-        pages_to(kv, 0)
-        page_in[kv][me] = page_out[kv, me]
+        pages_to(part, 0)
+        page_in[part][me] = page_out[part, me]
 
     def fresh_to(d):
         to = (me + d) % pools
@@ -208,39 +212,73 @@
         m_ref[rows, :] = m
         acc_ref[rows, :] = acc
 
-    def part_copy(kv, which):
+    def part_rows(part):
+        return pl.ds(pl.multiple_of(part * part_len, part_len), part_len)
+
+    def part_copy(half_at, which):
         part, peer = ((side, across), (side, by_pair), (across, by_pair))[which]
         return remote(
-            part_ref.at[part, kv],
-            part_ref.at[part, kv],
-            part_send.at[kv, which],
-            part_recv.at[kv, which],
+            part_ref.at[half_at, :, part_rows(part), :],
+            part_ref.at[half_at, :, part_rows(part), :],
+            part_send.at[half_at, which],
+            part_recv.at[half_at, which],
             "head",
             peer,
         )
 
-    def collect(kv):
-        each(1, pools, lambda d: page_copy(kv, d).wait())
-
-        def four(g, carry):
+    def collect(half_at):
+        each(1, pools, lambda d: page_copy(half_at, d).wait())
+        count = part_len // piece
+
+        def four(g):
             for j in range(4):
-                cell = cell_ref[g * 4 + j]
-                rows = pl.ds(pl.multiple_of((g * 4 + j) * piece, piece), piece)
-                part_ref[side, kv, rows, :] = page_in[kv][cell // bucket, cell % bucket]
-            return carry
-
-        lax.fori_loop(0, max_pages // 4, four, 0)
-        part_copy(kv, 0).start()
-        part_copy(kv, 1).start()
-
-    each(0, row_blocks * 5 // 8, new_rows)
-    collect(0)
-    each(row_blocks * 5 // 8, row_blocks, new_rows)
-    part_copy(0, 0).wait()
-    part_copy(0, 2).start()
-    collect(1)
-
-    each(1, pools, lambda d: fresh_copy(d).wait())
+                cell = cell_ref[half_at * count + g * 4 + j]
+                rows = pl.ds(pl.multiple_of(side * part_len + (g * 4 + j) * piece, piece), piece)
+                for kv in range(2):
+                    part_ref[half_at, kv, rows, :] = page_in[half_at][cell // bucket, cell % bucket, kv]
+
+        each(0, count // 4, four)
+        part_copy(half_at, 0).start()
+        part_copy(half_at, 1).start()
+
+    live_count, last_rank, tail = len_ref[0], len_ref[1], len_ref[2]
+
+    def finish(half_at, first):
+        part_copy(half_at, 1).wait()
+        part_copy(half_at, 2).wait()
+        if first is None:
+            first = part_ref[0, 0, 0:16, :].astype(jnp.float32)[0:1, :]
+        index = lax.broadcasted_iota(jnp.int32, (part_len, dim), 0)
+        rank = index // piece * 2 + half_at
+        for part in range(head_count):
+            rows = pl.ds(part * part_len, part_len)
+            row = part * piece + index % piece
+            live = (rank < live_count) & ((rank != last_rank) | (row < tail))
+            keys = part_ref[half_at, 0, rows, :].astype(jnp.float32)
+            part_ref[half_at, 0, rows, :] = jnp.where(live, keys, first).astype(jnp.bfloat16)
+            values = part_ref[half_at, 1, rows, :].astype(jnp.float32)
+            value_ref[half_at, rows, 0:dim] = jnp.where(live, values, 0.0).astype(jnp.bfloat16)
+            value_ref[half_at, rows, dim:] = jnp.where(live, 1.0, 0.0).astype(jnp.bfloat16)
+        return first
+
+    sub = row_block // 2
+
+    def prefix_rows(half_at, i):
+        both = [
+            pl.ds(pl.multiple_of(i * row_block + t * sub, sub), sub) for t in range(2)
+        ]
+        keys, values = part_ref[half_at, 0], value_ref[half_at]
+        scores = [
+            lax.dot_general(q_ref[rows, :], keys, (((1,), (1,)), ((), ())), preferred_element_type=jnp.float32)
+            for rows in both
+        ]
+        for rows, s in zip(both, scores):
+            m, acc = weigh(s, values, m_ref[rows, :], acc_ref[rows, :], scale)
+            if half_at == 0:
+                m_ref[rows, :] = m
+                acc_ref[rows, :] = acc
+            else:
+                out_ref[rows, :] = (acc[:, :dim] / acc[:, dim:]).astype(out_ref.dtype)
 
     def keep_page(s):
         at = place_smem[0, s]
@@ -250,49 +288,37 @@
             page = fresh_in[cell // bound, cell % bound, kv].astype(jnp.float32)
             stored_ref[s, kv, mine, :] = jnp.where(filled, page, 0.0).astype(jnp.bfloat16)
 
-    each(0, slots, keep_page)
-
     def stored_copy(which):
         part, peer = ((side, across), (side, by_pair), (across, by_pair))[which]
         rows = stored_ref.at[:, :, pl.ds(pl.multiple_of(part * piece, piece), piece), :]
         return remote(rows, rows, stored_send.at[which], stored_recv.at[which], "head", peer)
 
+    def forward(half_at):
+        part_copy(half_at, 0).wait()
+        part_copy(half_at, 2).start()
+
+    early = row_blocks * 3 // 4
+    each(0, early, new_rows)
+    collect(0)
+    each(early, row_blocks, new_rows)
+    forward(0)
+    first = finish(0, None)
+    each(0, row_blocks // 2, lambda i: prefix_rows(0, i))
+    collect(1)
+    each(row_blocks // 2, row_blocks * 7 // 8, lambda i: prefix_rows(0, i))
+    forward(1)
+    each(row_blocks * 7 // 8, row_blocks, lambda i: prefix_rows(0, i))
+    finish(1, first)
+    each(1, pools, lambda d: fresh_copy(d).wait())
+    each(0, slots, keep_page)
     stored_copy(0).start()
     stored_copy(1).start()
-    part_copy(1, 0).wait()
-    part_copy(1, 2).start()
+    each(0, row_blocks // 2, lambda i: prefix_rows(1, i))
     stored_copy(0).wait()
     stored_copy(2).start()
-    for which in (1, 2):
-        part_copy(0, which).wait()
-        part_copy(1, which).wait()
-
-    def stored_wait():
-        stored_copy(1).wait()
-        stored_copy(2).wait()
-
-    first = part_ref[0, 0, 0:16, :].astype(jnp.float32)[0:1, :]
-    index = lax.broadcasted_iota(jnp.int32, (part_len, dim), 0)
-    for part in range(head_count):
-        place = index // piece * page_len + part * piece + index % piece
-        live = place < len_ref[0]
-        keys = part_ref[part, 0].astype(jnp.float32)
-        part_ref[part, 0] = jnp.where(live, keys, first).astype(jnp.bfloat16)
-        values = part_ref[part, 1].astype(jnp.float32)
-        value_ref[part, :, 0:dim] = jnp.where(live, values, 0.0).astype(jnp.bfloat16)
-        value_ref[part, :, dim:] = jnp.where(live, 1.0, 0.0).astype(jnp.bfloat16)
-
-    def prefix_rows(i):
-        rows = pl.ds(pl.multiple_of(i * row_block, row_block), row_block)
-        q = q_ref[rows, :]
-        carry = (m_ref[rows, :], acc_ref[rows, :])
-        for part in range(head_count):
-            carry = absorb(q, part_ref[part, 0], value_ref[part], *carry, scale)
-        acc = carry[1]
-        out_ref[rows, :] = (acc[:, :dim] / acc[:, dim:]).astype(out_ref.dtype)
-
-    each(0, row_blocks, prefix_rows)
-    stored_wait()
+    each(row_blocks // 2, row_blocks, lambda i: prefix_rows(1, i))
+    stored_copy(1).wait()
+    stored_copy(2).wait()
 
 
 def fused(q, new_pairs, kv_pool, table, cells, source, length, slots, bucket, bound, pools, head_count, heads):
@@ -309,7 +335,7 @@
     )
     bf16, dma = jnp.bfloat16, pltpu.SemaphoreType.DMA
     smem, vmem = pl.BlockSpec(memory_space=pltpu.SMEM), pl.BlockSpec(memory_space=pltpu.VMEM)
-    part_len = max_pages * piece
+    half_len = max_pages // 2 * page_len
     return pl.pallas_call(
         kernel,
         out_shape=(
@@ -324,13 +350,13 @@
             pltpu.SMEM(table.shape, jnp.int32),
             pltpu.VMEM((1, 128), jnp.int32),
             pltpu.SMEM((1, 128), jnp.int32),
-            pltpu.VMEM((2, pools, bucket, piece, dim), bf16),
-            pltpu.VMEM((pools, bucket, piece, dim), bf16),
-            pltpu.VMEM((pools, bucket, piece, dim), bf16),
+            pltpu.VMEM((2, pools, bucket // 2, 2, piece, dim), bf16),
+            pltpu.VMEM((pools, bucket // 2, 2, piece, dim), bf16),
+            pltpu.VMEM((pools, bucket // 2, 2, piece, dim), bf16),
             pltpu.VMEM((pools, bound, 2, piece, dim), bf16),
             pltpu.VMEM((pools, bound, 2, piece, dim), bf16),
-            pltpu.VMEM((head_count, 2, part_len, dim), bf16),
-            pltpu.VMEM((head_count, part_len, 2 * dim), bf16),
+            pltpu.VMEM((2, 2, half_len, dim), bf16),
+            pltpu.VMEM((2, half_len, 2 * dim), bf16),
             pltpu.VMEM((new_pages * page_len, 2 * dim), bf16),
             pltpu.VMEM((rows, dim), jnp.float32),
             pltpu.VMEM((rows, 2 * dim), jnp.float32),
@@ -368,9 +394,25 @@
 
     live_pages = (length + page_len - 1) // page_len
     is_live = jnp.arange(max_pages, dtype=jnp.int32) < live_pages
-    prefix_cells, _, request_table = place_cells(
-        page_owner[0], page_slot[0], is_live, bucket, pool_count
-    )
+    owners = page_owner[0]
+    indices = jnp.arange(max_pages, dtype=jnp.int32)
+    same_owner = owners[:, None] == owners[None, :]
+    earlier = same_owner & (indices[:, None] > indices[None, :])
+    ahead = earlier | (owners[:, None] > owners[None, :])
+    position = jnp.sum(jnp.where(earlier & is_live[None, :], 1, 0), axis=1).astype(jnp.int32)
+    rank = jnp.sum(jnp.where(ahead & is_live[None, :], 1, 0), axis=1).astype(jnp.int32)
+    half_bucket = bucket // 2
+    cell = owners * bucket + rank % 2 * half_bucket + position // 2
+    cell = jnp.where(is_live, cell, -1)
+    cell_at = jnp.arange(pool_count * bucket, dtype=jnp.int32)
+    request_table = jnp.sum(
+        jnp.where(cell[:, None] == cell_at[None, :], page_slot[0][:, None], 0), axis=0
+    ).reshape(pool_count, bucket)
+    order = jnp.where(is_live, rank % 2 * (max_pages // 2) + rank // 2, -1)
+    half_cell = owners * half_bucket + position // 2
+    cells = jnp.sum(jnp.where(order[:, None] == indices[None, :], half_cell[:, None], 0), axis=0)
+    last_rank = jnp.sum(jnp.where(indices == live_pages - 1, rank, 0))
+    lengths = jnp.stack([live_pages, last_rank, length - (live_pages - 1) * page_len]).astype(jnp.int32)
     fresh_cells, fresh_matches, _ = place_cells(
         fresh_owner[0],
         fresh_slot[0],
@@ -381,10 +423,10 @@
     source = jnp.sum(
         jnp.where(fresh_matches, jnp.arange(new_count, dtype=jnp.int32)[:, None], 0), axis=0
     )
-    rank = fresh_cells % write_bound + lax.axis_index("pool") * write_bound + 1
+    stamp = fresh_cells % write_bound + lax.axis_index("pool") * write_bound + 1
     spot = fresh_owner[0] * 128 + fresh_slot[0]
     lanes = jnp.arange(pool_count * 128, dtype=jnp.int32)
-    places = jnp.sum(jnp.where(spot[:, None] == lanes[None, :], rank[:, None], 0), axis=0)
+    places = jnp.sum(jnp.where(spot[:, None] == lanes[None, :], stamp[:, None], 0), axis=0)
     table = jnp.stack(
         [jnp.pad(request_table, ((0, 0), (0, 128 - bucket))), places.reshape(pool_count, 128)], axis=1
     )
@@ -395,9 +437,9 @@
         new_pairs[0].reshape(2, new_count, page_len, dim),
         kv_pool,
         table,
-        jnp.maximum(prefix_cells, 0),
+        cells,
         source,
-        prefix_len,
+        lengths,
         fresh_total,
         bucket,
         write_bound,

time: 97.5 us -> 89.4 us (0.917)
  Pallas kernels: 85.2 us -> 74.1 us
  other arithmetic: 5.75 us -> 8.54 us
    pallas_call x1, Pallas kernels: 85.2 us -> 74.1 us  [fused(): pl.pallas_call(kernel, out_shape=(jax.ShapeDtypeStruct((rows, dim), bf16)...]
    reduce_sum x2 -> x4, other arithmetic: 0.84 us -> 2.36 us  [the longest x1 0.91 us: shards(): jnp.sum(jnp.where(earlier & is_live[None, :], 1, 0), axis=1)]
    select_n x0 -> x1, other arithmetic: none -> 1.39 us  [shards(): cell = jnp.where(is_live, cell, -1)]
    another operation x0 -> x1, other arithmetic: none -> 1.31 us  [shards(): jnp.stack([live_pages, last_rank, length - (live_pages - 1) * page_len])]
    max x1 -> x0, other arithmetic: 1.18 us -> none  [shards(): jnp.maximum(prefix_cells, 0)]
where the time goes in v3:
time: 89.4 us; the launch traced here: 89 us
  Pallas kernels  74.1 us (83%)
  other arithmetic  8.54 us (10%)
  local copies, waits for them, and re-layouts  4.96 us (6%)
  between operations  1.33 us (1%)
    pallas_call x1, Pallas kernels, fused(): pl.pallas_call(kernel, out_shape=(jax.ShapeDtypeStruct((rows, dim), bf16)...  74.1 us
    unnamed x2, local copies, waits for them, and re-layouts  4.88 us

profile of v3, /device:TPU:28, one launch (start us, length us, event | category | flops | bytes accessed | tf_op | source)
XLA Modules:
  0.0 89.0 jit_solution(16300924422068937391)
XLA Ops:
  1.3 0.9 %select_reduce_fusion.6 = s32[32]{0:T(128)S(1)} fusion(s32[32]{0:T(128)} %bitcast.27), kind=kLoop, calls=%fused_computation.12 | loop fusion | flops 5088 | bytes 256 | tf_op jit(solution)/shard_map/reduce_sum | solution.py:20
  2.2 0.7 fusion.4
  2.9 0.6 select_reduce_fusion.5.source_ref
  3.5 0.9 %select_reduce_fusion.3 = (s32[64]{0:T(128)S(1)}, s32[64]{0:T(128)S(1)}) fusion(s32[64]{0:T(128)} %bitcast.26, pred[64]{0:T(512)(128)(4,1)S(1)} %iota_compare_fusion.6), kind=kLoop, calls=%fused_computation.5 | loop fusion | flops 44928 | bytes 832 | tf_op jit(solution)/shard_map/reduce_sum | solution.py:402
  4.4 1.4 %add_select_fusion = (s32[64]{0:T(128)S(1)}, s32[64]{0:T(128)S(1)}, s32[64]{0:T(128)S(1)}, s32[]{:T(128)}) fusion(s32[1,64]{1,0:T(1,128)} %param.11, s32[64]{0:T(128)S(1)} %get-tuple-element.7, s32[]{:T(128)} %select_n.97, s32[64]{0:T(128)S(1)} %get-tuple-element.6, s32[]{:T(128)S(6)} %sub.28), kind=kLoop, calls=%fused_computation.35 | loop fusion | flops 2943 | bytes 1548 | tf_op jit(solution)/shard_map/jit(_where)/select_n | solution.py:406
  5.8 1.3 %pad_add_fusion.1.len_ref = s32[3]{0:T(128)} fusion(s32[1]{0:T(128)} %bitcast.4, s32[1]{0:T(128)} %bitcast.3, s32[1]{0:T(128)} %bitcast.1), kind=kLoop, calls=%fused_computation.33 | loop fusion | flops 6 | bytes 24 | tf_op jit(solution)/shard_map/stack | solution.py:415
  7.1 0.7 select_reduce_fusion.1
  7.9 0.7 multiply_add_fusion.1
  8.5 0.6 select_reduce_fusion.2.cell_ref
  9.2 0.1 select_reduce_fusion
  9.2 0.1 reshape.129
  9.3 0.6 pad_add_fusion.table_ref
  9.9 74.1 %shard_map.95 = (bf16[4096,128]{1,0:T(8,128)(2,1)}, bf16[32,2,64,128]{3,2,1,0:T(8,128)(2,1)}) custom-call(s32[3]{0:T(128)} %pad_add_fusion.1.len_ref, s32[64]{0:T(128)} %select_reduce_fusion.2.cell_ref, s32[32]{0:T(128)} %select_reduce_fusion.5.source_ref, s32[8,2,128]{2,1,0:T(2,128)} %pad_add_fusion.table_ref, bf16[4096,128]{1,0:T(8,128)(2,1)} %bitcast.22, ...), custom_call_target="tpu_custom_call" | custom-call | tf_op jit(solution)/shard_map/pallas_call | solution.py:339
  84.1 2.6 %copy.13 = bf16[1,2048,2,128]{3,2,1,0:T(2,128)(2,1)} copy(bf16[1,2048,2,128]{3,2,1,0:T(2,128)(2,1)} %bitcast.21) | data formatting | bytes 2097152
  86.6 2.3 %copy.14 = bf16[32,2,64,128]{3,2,1,0:T(8,128)(2,1)} copy(bf16[32,2,64,128]{3,2,1,0:T(8,128)(2,1)} %get-tuple-element.18) | data formatting | bytes 2097152
  (2 shorter events, 0.0 us)

commit v4 on v3

--- a/solution.py
+++ b/solution.py
@@ -165,8 +165,7 @@
         for c in range(bucket):
             page_out[part, to, c] = slice_ref[asked_smem[to, 0, part * bucket + c]]
 
-    for part in range(2):
-
+    def send_half(part):
         def send_pages(d):
             pages_to(part, d)
             page_copy(part, d).start()
@@ -174,6 +173,8 @@
         each(1, pools, send_pages)
         pages_to(part, 0)
         page_in[part][me] = page_out[part, me]
+
+    send_half(0)
 
     def fresh_to(d):
         to = (me + d) % pools
@@ -185,10 +186,6 @@
     def send_fresh(d):
         fresh_to(d)
         fresh_copy(d).start()
-
-    each(1, pools, send_fresh)
-    fresh_to(0)
-    fresh_in[me] = fresh_out[me]
 
     new_value_ref[:, 0:dim] = new_ref[1].reshape(new_pages * page_len, dim)
     new_value_ref[:, dim:] = jnp.ones((new_pages * page_len, dim), jnp.bfloat16)
@@ -298,10 +295,16 @@
         part_copy(half_at, 2).start()
 
     early = row_blocks * 3 // 4
-    each(0, early, new_rows)
+    each(0, row_blocks // 2, new_rows)
+    send_half(1)
+    each(row_blocks // 2, early, new_rows)
     collect(0)
-    each(early, row_blocks, new_rows)
+    each(1, pools, send_fresh)
+    fresh_to(0)
+    fresh_in[me] = fresh_out[me]
+    each(early, row_blocks - 1, new_rows)
     forward(0)
+    each(row_blocks - 1, row_blocks, new_rows)
     first = finish(0, None)
     each(0, row_blocks // 2, lambda i: prefix_rows(0, i))
     collect(1)

time: 89.4 us -> 87.7 us (0.981)
  Pallas kernels: 74.1 us -> 72.5 us
    pallas_call x1, Pallas kernels: 74.1 us -> 72.5 us  [fused(): pl.pallas_call(kernel, out_shape=(jax.ShapeDtypeStruct((rows, dim), bf16)...]
where the time goes in v4:
time: 87.7 us; the launch traced here: 87.4 us
  Pallas kernels  72.5 us (83%)
  other arithmetic  8.54 us (10%)
  local copies, waits for them, and re-layouts  4.96 us (6%)
  between operations  1.33 us (2%)
    pallas_call x1, Pallas kernels, fused(): pl.pallas_call(kernel, out_shape=(jax.ShapeDtypeStruct((rows, dim), bf16)...  72.5 us
    unnamed x2, local copies, waits for them, and re-layouts  4.88 us

profile of v4, /device:TPU:28, one launch (start us, length us, event | category | flops | bytes accessed | tf_op | source)
XLA Modules:
  0.0 87.4 jit_solution(1477048163262097592)
XLA Ops:
  1.3 0.9 %select_reduce_fusion.6 = s32[32]{0:T(128)S(1)} fusion(s32[32]{0:T(128)} %bitcast.27), kind=kLoop, calls=%fused_computation.12 | loop fusion | flops 5088 | bytes 256 | tf_op jit(solution)/shard_map/reduce_sum | solution.py:20
  2.2 0.7 fusion.4
  2.9 0.6 select_reduce_fusion.5.source_ref
  3.5 0.9 %select_reduce_fusion.3 = (s32[64]{0:T(128)S(1)}, s32[64]{0:T(128)S(1)}) fusion(s32[64]{0:T(128)} %bitcast.26, pred[64]{0:T(512)(128)(4,1)S(1)} %iota_compare_fusion.6), kind=kLoop, calls=%fused_computation.5 | loop fusion | flops 44928 | bytes 832 | tf_op jit(solution)/shard_map/reduce_sum | solution.py:405
  4.4 1.4 %add_select_fusion = (s32[64]{0:T(128)S(1)}, s32[64]{0:T(128)S(1)}, s32[64]{0:T(128)S(1)}, s32[]{:T(128)}) fusion(s32[1,64]{1,0:T(1,128)} %param.11, s32[64]{0:T(128)S(1)} %get-tuple-element.7, s32[]{:T(128)} %select_n.97, s32[64]{0:T(128)S(1)} %get-tuple-element.6, s32[]{:T(128)S(6)} %sub.28), kind=kLoop, calls=%fused_computation.35 | loop fusion | flops 2943 | bytes 1548 | tf_op jit(solution)/shard_map/jit(_where)/select_n | solution.py:409
  5.8 1.3 %pad_add_fusion.1.len_ref = s32[3]{0:T(128)} fusion(s32[1]{0:T(128)} %bitcast.4, s32[1]{0:T(128)} %bitcast.3, s32[1]{0:T(128)} %bitcast.1), kind=kLoop, calls=%fused_computation.33 | loop fusion | flops 6 | bytes 24 | tf_op jit(solution)/shard_map/stack | solution.py:418
  7.1 0.7 select_reduce_fusion.1
  7.9 0.7 multiply_add_fusion.1
  8.5 0.6 select_reduce_fusion.2.cell_ref
  9.2 0.1 select_reduce_fusion
  9.2 0.1 reshape.129
  9.3 0.6 pad_add_fusion.table_ref
  9.9 72.5 %shard_map.95 = (bf16[4096,128]{1,0:T(8,128)(2,1)}, bf16[32,2,64,128]{3,2,1,0:T(8,128)(2,1)}) custom-call(s32[3]{0:T(128)} %pad_add_fusion.1.len_ref, s32[64]{0:T(128)} %select_reduce_fusion.2.cell_ref, s32[32]{0:T(128)} %select_reduce_fusion.5.source_ref, s32[8,2,128]{2,1,0:T(2,128)} %pad_add_fusion.table_ref, bf16[4096,128]{1,0:T(8,128)(2,1)} %bitcast.22, ...), custom_call_target="tpu_custom_call" | custom-call | tf_op jit(solution)/shard_map/pallas_call | solution.py:342
  82.5 2.6 %copy.13 = bf16[1,2048,2,128]{3,2,1,0:T(2,128)(2,1)} copy(bf16[1,2048,2,128]{3,2,1,0:T(2,128)(2,1)} %bitcast.21) | data formatting | bytes 2097152
  85.1 2.3 %copy.14 = bf16[32,2,64,128]{3,2,1,0:T(8,128)(2,1)} copy(bf16[32,2,64,128]{3,2,1,0:T(8,128)(2,1)} %get-tuple-element.18) | data formatting | bytes 2097152
  (2 shorter events, 0.0 us)
